TPU v7x, 32 devices: a whole 2x2x4 slice. The times are simulated.
32 devices in a mesh: groups: 2 (over x), expert: 8 (over z, y), dp: 2 (over core).
Axes of the slice: x: 2, y: 2, z: 4, core: 2. Of those that a mesh axis runs over, the one named last changes fastest.
Arguments:
- tokens: bfloat16 [4096, 3584], P(('groups', 'expert', 'dp')), parts along dimension 0, may hold values from -6 to 6
- grad_out: bfloat16 [4096, 3584], P(('groups', 'expert', 'dp')), parts along dimension 0, may hold values from -6 to 6
- expert_ids: int32 [4096, 8], P(('groups', 'expert', 'dp')), parts along dimension 0, may hold values from 0 to 255, as said below
- gate_weights: float32 [4096, 8], P(('groups', 'expert', 'dp')), parts along dimension 0, may hold values from 0.05 to 0.6
- w_gate: bfloat16 [2048, 3584], P(('expert', 'dp')), may hold values from -0.09375 to 0.09375
- w_up: bfloat16 [2048, 3584], P(('expert', 'dp')), may hold values from -0.09375 to 0.09375
- w_down: bfloat16 [2048, 3584], P(('expert', 'dp')), may hold values from -0.1875 to 0.1875
Outputs:
- grad_tokens: bfloat16 [4096, 3584], P(('groups', 'expert', 'dp')), parts along dimension 0
- grad_gates: float32 [4096, 8], P(('groups', 'expert', 'dp')), parts along dimension 0
- grad_w_gate: bfloat16 [4096, 3584], P(('groups', 'expert', 'dp')), parts along dimension 0
- grad_w_up: bfloat16 [4096, 3584], P(('groups', 'expert', 'dp')), parts along dimension 0
- grad_w_down: bfloat16 [4096, 3584], P(('groups', 'expert', 'dp')), parts along dimension 0
There are 2 independent parts, one for each index of `groups`. A program takes and returns all parts, laid end to end along the dimension named above; an argument that names none is the same for every part. Nothing has to cross between parts.
Inputs may be any that keep to these rules, and one draw needn't show every extreme that they name: `expert_ids`: each row names 8 different experts. Each token names at most one expert below 2. Among the 128 rows of one device no expert below 2 is named by more than 6 rows, and on every device some such expert is named by exactly 6 rows.
All inputs are finite; a program needn't handle non-finite values.
Results may differ from a plain program's by a relative error of at most 0.017.
Values may be sent and summed in bfloat16 or wider, within the bound.
A program may use at most 128 MiB of HBM per device.

v0:
```python
import jax
import jax.numpy as jnp
from jax import lax
from jax.sharding import PartitionSpec as P

SPAN = 8
CAP = 6


def expert_pass(rows_x, rows_dy, rows_gate, w_gate, w_up, w_down):
    contract_last = (((1,), (1,)), ((), ()))
    contract_first = (((0,), (0,)), ((), ()))
    pre_gate = lax.dot_general(rows_x, w_gate, contract_last, preferred_element_type=jnp.float32)
    pre_up = lax.dot_general(rows_x, w_up, contract_last, preferred_element_type=jnp.float32)
    sigmoid_gate = jax.nn.sigmoid(pre_gate)
    hidden = (pre_gate * sigmoid_gate * pre_up).astype(jnp.bfloat16)
    partial_out = jnp.dot(hidden, w_down, preferred_element_type=jnp.float32)
    gate_dots = jnp.sum(rows_dy.astype(jnp.float32) * partial_out, axis=1)
    scaled = (rows_gate[:, None] * rows_dy.astype(jnp.float32)).astype(jnp.bfloat16)
    grad_hidden = lax.dot_general(scaled, w_down, contract_last, preferred_element_type=jnp.float32)
    grad_pre_gate = (
        grad_hidden * pre_up * sigmoid_gate * (1.0 + pre_gate * (1.0 - sigmoid_gate))
    ).astype(jnp.bfloat16)
    grad_pre_up = (grad_hidden * pre_gate * sigmoid_gate).astype(jnp.bfloat16)
    grad_down = lax.dot_general(
        hidden, scaled, contract_first, preferred_element_type=jnp.float32
    ).astype(jnp.bfloat16)
    grad_gate_w = lax.dot_general(
        grad_pre_gate, rows_x, contract_first, preferred_element_type=jnp.float32
    ).astype(jnp.bfloat16)
    grad_up_w = lax.dot_general(
        grad_pre_up, rows_x, contract_first, preferred_element_type=jnp.float32
    ).astype(jnp.bfloat16)
    partial_dx = jnp.dot(grad_pre_gate, w_gate, preferred_element_type=jnp.float32) + jnp.dot(
        grad_pre_up, w_up, preferred_element_type=jnp.float32
    )
    return (partial_dx, gate_dots, grad_gate_w, grad_up_w, grad_down)


def local(tokens, grad_out, expert_ids, gate_weights, w_gate, w_up, w_down):
    flat_count = lax.axis_size(("expert", "dp"))
    window_count = flat_count // SPAN
    features = tokens.shape[1]
    experts_here = jnp.arange(window_count, dtype=jnp.int32)
    matches = expert_ids[:, :, None] == experts_here[None, None, :]
    member = jnp.any(matches, axis=1)
    gate_sums = jnp.sum(jnp.where(matches, gate_weights[:, :, None], jnp.float32(0.0)), axis=1)
    slot_rank = jnp.cumsum(member.astype(jnp.int32), axis=0) - 1
    slot_ids = jnp.arange(CAP, dtype=jnp.int32)
    picker = member.T[:, None, :] & (slot_rank.T[:, None, :] == slot_ids[None, :, None])
    picker_half = picker.astype(jnp.bfloat16)
    picker_full = picker.astype(jnp.float32)
    send_x = jnp.einsum(
        "krt,td->krd", picker_half, tokens, preferred_element_type=jnp.float32
    ).astype(jnp.bfloat16)
    send_dy = jnp.einsum(
        "krt,td->krd", picker_half, grad_out, preferred_element_type=jnp.float32
    ).astype(jnp.bfloat16)
    send_gate = jnp.einsum("krt,tk->kr", picker_full, gate_sums, precision=lax.Precision.HIGHEST)
    got_x, got_dy, got_gate = (
        lax.all_to_all(
            jnp.repeat(send_x, SPAN, axis=0),
            ("expert", "dp"),
            split_axis=0,
            concat_axis=0,
            tiled=True,
        ),
        lax.all_to_all(
            jnp.repeat(send_dy, SPAN, axis=0),
            ("expert", "dp"),
            split_axis=0,
            concat_axis=0,
            tiled=True,
        ),
        lax.all_to_all(
            jnp.repeat(send_gate, SPAN, axis=0).astype(jnp.bfloat16),
            ("expert", "dp"),
            split_axis=0,
            concat_axis=0,
            tiled=True,
        ).astype(jnp.float32),
    )
    partial_dx, gate_dots, grad_gate_w, grad_up_w, grad_down = expert_pass(
        got_x.reshape(-1, features),
        got_dy.reshape(-1, features),
        got_gate.reshape(-1),
        w_gate,
        w_up,
        w_down,
    )
    back_dx, back_dots = (
        lax.all_to_all(
            partial_dx.reshape(flat_count, CAP, features).astype(jnp.bfloat16),
            ("expert", "dp"),
            split_axis=0,
            concat_axis=0,
            tiled=True,
        ).astype(jnp.float32),
        lax.all_to_all(
            gate_dots.reshape(flat_count, CAP).astype(jnp.bfloat16),
            ("expert", "dp"),
            split_axis=0,
            concat_axis=0,
            tiled=True,
        ).astype(jnp.float32),
    )
    total_dx = jnp.sum(back_dx.reshape(window_count, SPAN, CAP, features), axis=1)
    total_dots = jnp.sum(back_dots.reshape(window_count, SPAN, CAP), axis=1)
    grad_tokens = jnp.einsum(
        "krt,krd->td", picker_full, total_dx, precision=lax.Precision.HIGHEST
    ).astype(jnp.bfloat16)
    token_dots = jnp.einsum("krt,kr->tk", picker_full, total_dots, precision=lax.Precision.HIGHEST)
    grad_gates = jnp.sum(jnp.where(matches, token_dots[:, None, :], jnp.float32(0.0)), axis=2)
    return (grad_tokens, grad_gates, grad_gate_w, grad_up_w, grad_down)


def solution(mesh):
    in_specs = (
        P(("groups", "expert", "dp"), None),
        P(("groups", "expert", "dp"), None),
        P(("groups", "expert", "dp"), None),
        P(("groups", "expert", "dp"), None),
        P(("expert", "dp"), None),
        P(("expert", "dp"), None),
        P(("expert", "dp"), None),
    )
    out_specs = (
        P(("groups", "expert", "dp"), None),
        P(("groups", "expert", "dp"), None),
        P(("groups", "expert", "dp"), None),
        P(("groups", "expert", "dp"), None),
        P(("groups", "expert", "dp"), None),
    )
    return jax.shard_map(local, mesh=mesh, in_specs=in_specs, out_specs=out_specs, check_vma=False)
```

profile of v0, /device:TPU:0, one launch (start us, length us, event | category | flops | bytes accessed | tf_op | source)
XLA Modules:
  0.0 120.9 jit_solution(7414229896619092966)
XLA Ops:
  0.6 0.8 fusion.5
  1.6 0.2 reduce_window_sum.11
  1.8 1.4 %convolution_convert_fusion.3 = bf16[2,6,3584]{2,1,0:T(8,128)(2,1)S(1)} fusion(bf16[128,3584]{1,0:T(8,128)(2,1)} %param.7, s32[2,128]{1,0:T(2,128)S(1)} %copy.37, pred[2,128]{1,0:T(4,128)(4,1)S(1)} %bitcast.54), kind=kOutput, calls=%fused_computation.8 | convolution fusion | flops 11056128 | bytes 1004800 | tf_op jit(solution)/shard_map/krt,td->krd/dot_general | solution.py:53
  3.2 1.0 broadcast_in_dim.42
  4.2 7.4 %all-to-all-start.2 = ((bf16[16,6,3584]{2,1,0:T(8,128)(2,1)}), bf16[16,6,3584]{2,1,0:T(8,128)(2,1)S(1)}, u32[]{:S(2)}, u32[]{:S(2)}) async-start(bf16[16,6,3584]{2,1,0:T(8,128)(2,1)} %bitcast.8), calls=%async_computation.2 | async-start | bytes 1835008 | tf_op jit(solution)/shard_map/all_to_all | solution.py:61
  11.6 0.2 convolution_convert_fusion.4
  11.8 20.6 %all-to-all-done.2 = bf16[16,6,3584]{2,1,0:T(8,128)(2,1)S(1)} async-done(((bf16[16,6,3584]{2,1,0:T(8,128)(2,1)}), bf16[16,6,3584]{2,1,0:T(8,128)(2,1)S(1)}, u32[]{:S(2)}, u32[]{:S(2)}) %all-to-all-start.2) | async-done | bytes 688160 | tf_op jit(solution)/shard_map/all_to_all | solution.py:61
  32.4 1.1 broadcast_in_dim.41
  33.5 0.2 copy-done.3
  33.7 6.4 %all-to-all-start.1 = ((bf16[16,6,3584]{2,1,0:T(8,128)(2,1)}), bf16[16,6,3584]{2,1,0:T(8,128)(2,1)}, u32[]{:S(2)}, u32[]{:S(2)}) async-start(bf16[16,6,3584]{2,1,0:T(8,128)(2,1)} %bitcast.52), calls=%async_computation.1 | async-start | bytes 1835008 | tf_op jit(solution)/shard_map/all_to_all | solution.py:68
  40.0 1.4 %reshape.76 = bf16[96,3584]{1,0:T(8,128)(2,1)S(1)} reshape(bf16[16,6,3584]{2,1,0:T(8,128)(2,1)} %copy-done.3) | data formatting | bytes 1376256 | tf_op jit(solution)/shard_map/reshape | solution.py:84
  41.4 0.4 fusion.25
  41.8 0.4 multiply_convert_fusion.1
  42.3 18.6 %all-to-all-done.1 = bf16[16,6,3584]{2,1,0:T(8,128)(2,1)} async-done(((bf16[16,6,3584]{2,1,0:T(8,128)(2,1)}), bf16[16,6,3584]{2,1,0:T(8,128)(2,1)}, u32[]{:S(2)}, u32[]{:S(2)}) %all-to-all-start.1) | async-done | bytes 688160 | tf_op jit(solution)/shard_map/all_to_all | solution.py:68
  60.9 1.3 %reshape.80 = f32[96,3584]{1,0:T(8,128)S(1)} reshape(bf16[16,6,3584]{2,1,0:T(8,128)(2,1)} %all-to-all-done.1) | data formatting | bytes 2064384 | tf_op jit(solution)/shard_map/convert_element_type | solution.py:19
  62.3 1.6 %fusion.2 = bf16[96]{0:T(256)(128)(2,1)S(1)} fusion(f32[96,3584]{1,0:T(8,128)S(1)} %reshape.80, bf16[96,128]{1,0:T(8,128)(2,1)S(1)} %get-tuple-element.9, bf16[128,3584]{1,0:T(8,128)(2,1)} %param.13), kind=kOutput, calls=%fused_computation.12 | convolution fusion | flops 88768416 | bytes 2318528 | tf_op jit(solution)/shard_map/dot_general | solution.py:17
  64.0 12.4 %all_to_all.27 = bf16[16,1,6]{2,1,0:T(2,128)(2,1)S(1)} all-to-all(bf16[16,1,6]{2,1,0:T(2,128)(2,1)S(1)} %convert_element_type.123), channel_id=1, replica_groups=mesh['groups'=2,'expert'=8,'dp'=2] {'expert','dp'}, dimensions={0} | all-to-all | bytes 384 | tf_op jit(solution)/shard_map/all_to_all | solution.py:99
  76.8 0.1 fusion.7
  76.9 0.6 select_reduce_fusion
  77.5 0.1 fusion.12
  78.0 9.0 %all_to_all.28 = bf16[16,1,6]{2,1,0:T(2,128)(2,1)S(1)} all-to-all(bf16[16,1,6]{2,1,0:T(2,128)(2,1)S(1)} %copy.38), channel_id=1, replica_groups=mesh['groups'=2,'expert'=8,'dp'=2] {'expert','dp'}, dimensions={0} | all-to-all | bytes 384 | tf_op jit(solution)/shard_map/all_to_all | solution.py:75
  87.1 1.7 %multiply_convert_fusion.2 = (bf16[96,128]{1,0:T(8,128)(2,1)S(1)}, bf16[96,128]{1,0:T(8,128)(2,1)S(1)}) fusion(f32[96,128]{1,0:T(8,128)S(1)} %fusion.25, f32[96,128]{1,0:T(8,128)S(1)} %get-tuple-element.10, bf16[128,3584]{1,0:T(8,128)(2,1)} %param.13, f32[96,3584]{1,0:T(8,128)S(1)} %reshape.80, f32[96]{0:T(128)S(1)} %reshape.79), kind=kOutput, calls=%fused_computation.17 | convolution fusion | flops 88928256 | bytes 2441600 | tf_op jit(solution)/shard_map/dot_general | solution.py:20
  88.8 0.3 fusion.26
  89.2 1.2 fusion.1
  90.4 2.1 %convert_element_type.110 = bf16[16,6,3584]{2,1,0:T(8,128)(2,1)} reshape(bf16[96,3584]{1,0:T(8,128)(2,1)} %fusion.1) | data formatting | bytes 1376256 | tf_op jit(solution)/shard_map/convert_element_type | solution.py:93
  92.5 4.3 %all-to-all-start.3 = ((bf16[16,6,3584]{2,1,0:T(8,128)(2,1)}), bf16[16,6,3584]{2,1,0:T(8,128)(2,1)}, u32[]{:S(2)}, u32[]{:S(2)}) async-start(bf16[16,6,3584]{2,1,0:T(8,128)(2,1)} %convert_element_type.110), calls=%async_computation.3 | async-start | bytes 1835008 | tf_op jit(solution)/shard_map/all_to_all | solution.py:92
  96.8 1.3 %convolution_convert_fusion.1 = bf16[128,3584]{1,0:T(8,128)(2,1)} fusion(bf16[96,128]{1,0:T(8,128)(2,1)S(1)} %get-tuple-element.7, bf16[96,3584]{1,0:T(8,128)(2,1)S(1)} %reshape.76), kind=kOutput, calls=%fused_computation.5 | convolution fusion | flops 88539136 | bytes 1630208 | tf_op jit(solution)/shard_map/dot_general | solution.py:31
  98.2 1.3 %convolution_convert_fusion.2 = bf16[128,3584]{1,0:T(8,128)(2,1)} fusion(bf16[96,128]{1,0:T(8,128)(2,1)S(1)} %get-tuple-element.8, bf16[96,3584]{1,0:T(8,128)(2,1)S(1)} %reshape.76), kind=kOutput, calls=%fused_computation.6 | convolution fusion | flops 88539136 | bytes 1630208 | tf_op jit(solution)/shard_map/dot_general | solution.py:28
  99.5 1.4 %convolution_convert_fusion = bf16[128,3584]{1,0:T(8,128)(2,1)} fusion(bf16[96,128]{1,0:T(8,128)(2,1)S(1)} %get-tuple-element.9, f32[96,3584]{1,0:T(8,128)S(1)} %reshape.80, f32[96]{0:T(128)S(1)} %reshape.79), kind=kOutput, calls=%fused_computation.4 | convolution fusion | flops 89227264 | bytes 2318720 | tf_op jit(solution)/shard_map/dot_general | solution.py:25
  100.9 16.7 %all-to-all-done.3 = bf16[16,6,3584]{2,1,0:T(8,128)(2,1)} async-done(((bf16[16,6,3584]{2,1,0:T(8,128)(2,1)}), bf16[16,6,3584]{2,1,0:T(8,128)(2,1)}, u32[]{:S(2)}, u32[]{:S(2)}) %all-to-all-start.3) | async-done | bytes 688160 | tf_op jit(solution)/shard_map/all_to_all | solution.py:92
  117.6 1.4 %convert_reduce_fusion = f32[2,6,3584]{2,1,0:T(8,128)S(1)} fusion(bf16[16,6,3584]{2,1,0:T(8,128)(2,1)} %all-to-all-done.3), kind=kLoop, calls=%fused_computation.10 | loop fusion | flops 645120 | bytes 860160 | tf_op jit(solution)/shard_map/reduce_sum | solution.py:107
  119.0 1.9 %fusion = bf16[128,3584]{1,0:T(8,128)(2,1)} fusion(f32[2,6,3584]{2,1,0:T(8,128)S(1)} %convert_reduce_fusion, s32[2,128]{1,0:T(2,128)S(1)} %copy.37, pred[2,128]{1,0:T(4,128)(4,1)S(1)} %bitcast.58), kind=kOutput, calls=%fused_computation.3 | convolution fusion | flops 66522112 | bytes 1090816 | tf_op jit(solution)/shard_map/krt,krd->td/dot_general | solution.py:109
  (29 shorter events, 1.2 us)
Async XLA Ops:
  0.6 41.2 %copy-start = (bf16[128,3584]{1,0:T(8,128)(2,1)S(1)}, bf16[128,3584]{1,0:T(8,128)(2,1)}, u32[]{:S(2)}) copy-start(bf16[128,3584]{1,0:T(8,128)(2,1)} %param.12) | copy-start | bytes 2752516
  3.2 8.4 %copy-start.4 = (bf16[128,3584]{1,0:T(8,128)(2,1)S(1)}, bf16[128,3584]{1,0:T(8,128)(2,1)}, u32[]{:S(2)}) copy-start(bf16[128,3584]{1,0:T(8,128)(2,1)} %param.8) | copy-start | bytes 2752516
  4.2 28.2 %all-to-all-start.2 = ((bf16[16,6,3584]{2,1,0:T(8,128)(2,1)}), bf16[16,6,3584]{2,1,0:T(8,128)(2,1)S(1)}, u32[]{:S(2)}, u32[]{:S(2)}) async-start(bf16[16,6,3584]{2,1,0:T(8,128)(2,1)} %bitcast.8), calls=%async_computation.2 | async-start | bytes 1835008 | tf_op jit(solution)/shard_map/all_to_all | solution.py:61
  32.4 1.2 %copy-start.3 = (bf16[16,6,3584]{2,1,0:T(8,128)(2,1)}, bf16[16,6,3584]{2,1,0:T(8,128)(2,1)S(1)}, u32[]{:S(2)}) copy-start(bf16[16,6,3584]{2,1,0:T(8,128)(2,1)S(1)} %all-to-all-done.2) | copy-start | bytes 2064388
  33.7 7.8 %copy-start.1 = (bf16[128,3584]{1,0:T(8,128)(2,1)S(1)}, bf16[128,3584]{1,0:T(8,128)(2,1)}, u32[]{:S(2)}) copy-start(bf16[128,3584]{1,0:T(8,128)(2,1)} %param.11) | copy-start | bytes 2752516
  33.7 27.2 %all-to-all-start.1 = ((bf16[16,6,3584]{2,1,0:T(8,128)(2,1)}), bf16[16,6,3584]{2,1,0:T(8,128)(2,1)}, u32[]{:S(2)}, u32[]{:S(2)}) async-start(bf16[16,6,3584]{2,1,0:T(8,128)(2,1)} %bitcast.52), calls=%async_computation.1 | async-start | bytes 1835008 | tf_op jit(solution)/shard_map/all_to_all | solution.py:68
  62.2 14.7 %copy-start.5 = (s32[128,8]{0,1:T(8,128)S(1)}, s32[128,8]{0,1:T(8,128)}, u32[]{:S(2)}) copy-start(s32[128,8]{0,1:T(8,128)} %param.9) | copy-start | bytes 12292
  62.2 14.6 %copy-start.6 = (f32[128,8]{0,1:T(8,128)S(1)}, f32[128,8]{0,1:T(8,128)}, u32[]{:S(2)}) copy-start(f32[128,8]{0,1:T(8,128)} %param.10) | copy-start | bytes 12292
  87.1 1.7 %copy-start.2 = (bf16[128,3584]{1,0:T(8,128)(2,1)S(1)}, bf16[128,3584]{1,0:T(8,128)(2,1)}, u32[]{:S(2)}) copy-start(bf16[128,3584]{1,0:T(8,128)(2,1)} %param.11) | copy-start | bytes 2752516
  92.5 25.1 %all-to-all-start.3 = ((bf16[16,6,3584]{2,1,0:T(8,128)(2,1)}), bf16[16,6,3584]{2,1,0:T(8,128)(2,1)}, u32[]{:S(2)}, u32[]{:S(2)}) async-start(bf16[16,6,3584]{2,1,0:T(8,128)(2,1)} %convert_element_type.110), calls=%async_computation.3 | async-start | bytes 1835008 | tf_op jit(solution)/shard_map/all_to_all | solution.py:92
where the time goes:
time: 122 us; the launch traced here: 121 us
  waiting for transfers between devices  55.9 us (46%)
  blocking collectives  21.4 us (18%)
  starting transfers between devices  18 us (15%)
  matrix products  13.6 us (11%)
  local copies, waits for them, and re-layouts  8.1 us (7%)
  other arithmetic  3.08 us (3%)
    all_to_all x1, waiting for transfers between devices, local(): lax.all_to_all(jnp.repeat(send_x, SPAN, axis=0), ('expert', 'dp'), split_...  20.6 us
    all_to_all x1, waiting for transfers between devices, local(): lax.all_to_all(jnp.repeat(send_dy, SPAN, axis=0), ('expert', 'dp'), split...  18.6 us
    all_to_all x1, waiting for transfers between devices, local(): lax.all_to_all(partial_dx.reshape(flat_count, CAP, features).astype(jnp.b...  16.7 us
    all_to_all x1, blocking collectives, local(): lax.all_to_all(gate_dots.reshape(flat_count, CAP).astype(jnp.bfloat16), (...  12.4 us
    all_to_all x1, blocking collectives, local(): lax.all_to_all(jnp.repeat(send_gate, SPAN, axis=0).astype(jnp.bfloat16),...  8.97 us
    all_to_all x1, starting transfers between devices, local(): lax.all_to_all(jnp.repeat(send_x, SPAN, axis=0), ('expert', 'dp'), split_...  7.39 us
    all_to_all x1, starting transfers between devices, local(): lax.all_to_all(jnp.repeat(send_dy, SPAN, axis=0), ('expert', 'dp'), split...  6.35 us
    all_to_all x1, starting transfers between devices, local(): lax.all_to_all(partial_dx.reshape(flat_count, CAP, features).astype(jnp.b...  4.31 us
  transfers between devices with their start and end apart: 3, of which 3 were waited for; matrix products, arithmetic and copies ran while one was open for 5% of the time, Pallas kernels for 0%

commit v1 on v0

v1 whole, which is shorter than its diff:
```python
import functools

import jax
import jax.numpy as jnp
from jax import lax
from jax.experimental import pallas as pl
from jax.experimental.pallas import tpu as pltpu
from jax.sharding import PartitionSpec as P

SPAN = 8
CAP = 6
ROWS = 16
LANE = 128
FIRST = (((0,), (0,)), ((), ()))
LAST = (((1,), (1,)), ((), ()))
F32 = jnp.float32
BF16 = jnp.bfloat16


def loop(count, body):
    if count <= 2:
        for i in range(count):
            body(i)
    else:
        pl.loop(0, count)(body)


def exchange_kernel(
    experts,
    tokens_ref, grad_ref, ids_ref, gates_ref, wg_ref, wu_ref, wd_ref,
    buf, act_ref, sel_ref, fin,
    tok_v, dy_v, w_v, send, dxb, rc, r2, r1,
    in_sem, s1_s, s1_r, a1_s, a1_r, a2_s, a2_r, a3_s, a3_r, ac_s, ac_r,
    rc_s, rc_r, r2_s, r2_r, r1_s, r1_r, r0_s, r0_r,
):
    features = tok_v.shape[1]
    half = features // 2
    hid = wg_ref.shape[0]
    dp = lax.axis_index("dp")
    flat = lax.axis_index("expert") * 2 + dp
    octet = flat // SPAN
    pos = flat % SPAN
    bit1 = (pos // 2) % 2
    bit2 = pos // 4
    step2 = 2 - 4 * bit1
    step4 = 4 - 8 * bit2
    step_c = 1 - 2 * dp
    first = jnp.where(dp == 0, step4, step2)
    second = jnp.where(dp == 0, step2, step4)

    def dev(index):
        return {"expert": index // 2, "dp": index % 2}

    barrier = pltpu.get_barrier_semaphore()
    for step in (first, second, step_c):
        pl.semaphore_signal(barrier, 1, device_id=dev(flat + step), device_id_type=pl.DeviceIdType.MESH)

    def greet(i):
        other = lax.rem(octet + i + 1, experts) * SPAN + pos
        pl.semaphore_signal(barrier, 1, device_id=dev(other), device_id_type=pl.DeviceIdType.MESH)

    loop(experts - 1, greet)

    loads = [
        pltpu.make_async_copy(tokens_ref, tok_v, in_sem.at[0]),
        pltpu.make_async_copy(grad_ref, dy_v, in_sem.at[1]),
        pltpu.make_async_copy(wg_ref, w_v.at[pl.ds(0, hid)], in_sem.at[2]),
        pltpu.make_async_copy(wu_ref, w_v.at[pl.ds(hid, hid)], in_sem.at[3]),
        pltpu.make_async_copy(wd_ref, w_v.at[pl.ds(2 * hid, hid)], in_sem.at[4]),
    ]
    for copy in loads:
        copy.start()

    count = ids_ref.shape[0]
    width = experts * ROWS
    lane = lax.broadcasted_iota(jnp.int32, (count, width), 1)
    lane_expert = lane // ROWS
    lane_row = lane % 8
    lane_dy = (lane // 8) % 2
    member = jnp.zeros((count, width), F32)
    gate = jnp.zeros((count, width), F32)
    for s in range(ids_ref.shape[1]):
        hit = ids_ref[:, s : s + 1] == lane_expert
        member = member + jnp.where(hit, 1.0, 0.0)
        gate = gate + jnp.where(hit, gates_ref[:, s : s + 1], 0.0)
    lower = jnp.where(
        lax.broadcasted_iota(jnp.int32, (count, count), 0)
        >= lax.broadcasted_iota(jnp.int32, (count, count), 1),
        1.0, 0.0,
    ).astype(BF16)
    rank = jnp.dot(lower, member.astype(BF16), preferred_element_type=F32)
    chosen = jnp.where(
        (member > 0.5) & (rank == (lane_row + 1).astype(F32)) & (lane_row < CAP), 1.0, 0.0
    )
    sel_x = jnp.where(lane_dy == 0, chosen, 0.0)
    sel_dy = jnp.where(lane_dy == 1, chosen, 0.0)
    gate_hi = gate.astype(BF16).astype(F32)
    gate_mix = (sel_x * gate_hi + sel_dy * (gate - gate_hi)).astype(BF16)
    sel_x = sel_x.astype(BF16)
    sel_dy = sel_dy.astype(BF16)
    sel_ref[0] = sel_x
    sel_ref[1] = sel_dy
    send[:, :, features:] = (
        lax.dot_general(gate_mix, jnp.ones((count, LANE), BF16), FIRST, preferred_element_type=F32)
        .astype(BF16)
        .reshape(experts, ROWS, LANE)
    )
    loads[0].wait()
    loads[1].wait()
    tile = features // 4
    for c in range(4):
        cols = pl.ds(c * tile, tile)
        block = lax.dot_general(
            sel_x, tok_v[:, cols], FIRST, preferred_element_type=F32
        ) + lax.dot_general(sel_dy, dy_v[:, cols], FIRST, preferred_element_type=F32)
        send[:, :, cols] = block.astype(BF16).reshape(experts, ROWS, tile)
    buf[flat] = send[octet]
    pl.semaphore_wait(barrier, 3 + experts - 1)

    def remote(src, dst, ssem, rsem, index):
        return pltpu.make_async_remote_copy(
            src_ref=src, dst_ref=dst, send_sem=ssem, recv_sem=rsem,
            device_id=dev(index), device_id_type=pl.DeviceIdType.MESH,
        )

    def source(d):
        return lax.rem(octet - d + experts, experts)

    def s1(i):
        other = lax.rem(octet + i + 1, experts)
        return remote(send.at[other], buf.at[flat], s1_s.at[i], s1_r.at[i], other * SPAN + pos)

    def pass_on(slot, ssem, rsem, index):
        return remote(buf.at[slot], buf.at[slot], ssem, rsem, index)

    def base(d):
        return source(d) * SPAN + pos

    def a1(d):
        return pass_on(base(d), a1_s.at[d], a1_r.at[d], flat + first)

    def a2(d):
        return pass_on(base(d), a2_s.at[d], a2_r.at[d], flat + second)

    def a3(d):
        return pass_on(base(d) + first, a3_s.at[d], a3_r.at[d], flat + second)

    offsets = (0, first, second, first + second)

    def ac(d, k):
        return pass_on(base(d) + offsets[k], ac_s.at[d, k], ac_r.at[d, k], flat + step_c)

    def own(d):
        a1(d).start()
        a2(d).start()
        ac(d, 0).start()

    loop(experts - 1, lambda i: s1(i).start())
    own(0)

    def after_s1(i):
        s1(i).wait_recv()
        own(i + 1)

    def after_a1(d):
        a1(d).wait_recv()
        a3(d).start()
        ac(d, 1).start()

    def after_a2(d):
        a2(d).wait_recv()
        ac(d, 2).start()

    def after_a3(d):
        a3(d).wait_recv()
        ac(d, 3).start()

    after_a1(0)
    after_a2(0)
    loop(experts - 1, after_s1)
    after_a3(0)

    def rest(i):
        after_a1(i + 1)
        after_a2(i + 1)

    loop(experts - 1, rest)
    loop(experts - 1, lambda i: after_a3(i + 1))
    for copy in loads[2:]:
        copy.wait()

    def all_core(d):
        for k in range(4):
            ac(d, k).wait_recv()

    loop(experts, all_core)

    def compute(f):
        rows = pl.ds(f * SPAN, SPAN)
        total = jnp.zeros((SPAN * ROWS, 3 * hid), F32)
        for c in range(4):
            cols = pl.ds(c * tile, tile)
            total = total + lax.dot_general(
                buf[rows, :, cols].reshape(SPAN * ROWS, tile), w_v[:, cols], LAST,
                preferred_element_type=F32,
            )
        total = total.reshape(SPAN, 2, 8, 3 * hid)
        from_x = total[:, 0].reshape(SPAN * 8, 3 * hid)
        from_dy = total[:, 1].reshape(SPAN * 8, 3 * hid)
        pre_gate = from_x[:, :hid]
        pre_up = from_x[:, hid : 2 * hid]
        back = from_dy[:, 2 * hid :]
        packed = buf[rows, :, pl.ds(features, LANE)].astype(F32)
        weight = (packed[:, :8] + packed[:, 8:]).reshape(SPAN * 8, LANE)
        sig = jax.nn.sigmoid(pre_gate)
        silu = pre_gate * sig
        hidden = silu * pre_up
        dots = jnp.sum(hidden.astype(BF16).astype(F32) * back, axis=1, keepdims=True)
        grad_hidden = back * weight
        grad_gate = grad_hidden * pre_up * sig * (1.0 + pre_gate * (1.0 - sig))
        grad_up = grad_hidden * silu
        down = (hidden * weight).reshape(SPAN, 8, hid)
        none = jnp.zeros((SPAN, 8, hid), F32)
        upper = jnp.concatenate([grad_gate.reshape(SPAN, 8, hid), grad_up.reshape(SPAN, 8, hid), none], axis=2)
        under = jnp.concatenate([none, none, down], axis=2)
        act_ref[rows] = jnp.concatenate([upper, under], axis=1).astype(BF16)
        pair = jnp.concatenate([grad_gate, grad_up], axis=1).astype(BF16)
        spread = jnp.broadcast_to(dots, (SPAN * 8, LANE)).reshape(SPAN, 8, LANE)
        dxb[rows, :, pl.ds(half, LANE)] = jnp.concatenate([spread, spread], axis=1).astype(BF16)
        step = half // 2
        for c in range(2):
            left = jnp.dot(pair, w_v[: 2 * hid, c * step : (c + 1) * step], preferred_element_type=F32)
            right = jnp.dot(
                pair, w_v[: 2 * hid, half + c * step : half + (c + 1) * step], preferred_element_type=F32
            )
            dxb[rows, :, pl.ds(c * step, step)] = jnp.concatenate(
                [left.reshape(SPAN, 8, step), right.reshape(SPAN, 8, step)], axis=1
            ).astype(BF16)

    loop(experts, compute)

    partner_offsets = (0, second, first, first + second)

    def back_core(d, k):
        return remote(
            dxb.at[base(d) + step_c + partner_offsets[k]], rc.at[d, k], rc_s.at[d, k], rc_r.at[d, k], flat + step_c
        )

    def back_second(d, k):
        return remote(
            dxb.at[base(d) + second + (0, first)[k]], r2.at[d, k], r2_s.at[d, k], r2_r.at[d, k], flat + second
        )

    def back_first(d):
        return remote(dxb.at[base(d) + first], r1.at[d], r1_s.at[d], r1_r.at[d], flat + first)

    def home(i):
        to = source(i + 1)
        return remote(dxb.at[base(i + 1)], fin.at[octet], r0_s.at[i], r0_r.at[i], to * SPAN + pos)

    def add(slot, piece):
        dxb[slot] = (dxb[slot].astype(F32) + piece.astype(F32)).astype(BF16)

    def start_core(i):
        d = experts - 1 - i
        for k in (2, 3, 1, 0):
            back_core(d, k).start()

    loop(experts, start_core)

    def sum_core(i):
        d = experts - 1 - i
        for k in (2, 3):
            back_core(d, k).wait_recv()
            add(base(d) + offsets[k], rc[d, k])
            back_second(d, k - 2).start()
        for k in (1, 0):
            back_core(d, k).wait_recv()
            add(base(d) + offsets[k], rc[d, k])

    loop(experts, sum_core)

    def sum_second(i):
        d = experts - 1 - i
        back_second(d, 1).wait_recv()
        add(base(d) + first, r2[d, 1])
        back_first(d).start()
        back_second(d, 0).wait_recv()
        add(base(d), r2[d, 0])

    loop(experts, sum_second)

    def sum_first(i):
        d = experts - 1 - i
        back_first(d).wait_recv()
        add(base(d), r1[d])
        home(d - 1).start()

    loop(experts - 1, sum_first)
    back_first(0).wait_recv()
    fin[octet] = (dxb[flat].astype(F32) + r1[0].astype(F32)).astype(BF16)
    loop(experts - 1, lambda i: home(i).wait_recv())

    def finish(d):
        a1(d).wait_send()
        a2(d).wait_send()
        a3(d).wait_send()
        back_first(d).wait_send()
        for k in range(4):
            ac(d, k).wait_send()
            back_core(d, k).wait_send()
        for k in range(2):
            back_second(d, k).wait_send()

    loop(experts, finish)

    def finish_far(i):
        s1(i).wait_send()
        home(i).wait_send()

    loop(experts - 1, finish_far)


def output_kernel(
    experts, buf_ref, act_ref, sel_ref, fin_ref, dots_ref, ids_ref,
    gt_ref, gg_ref, wg_ref, wu_ref, wd_ref,
):
    hid = wg_ref.shape[0]
    grads = lax.dot_general(act_ref[...], buf_ref[...], FIRST, preferred_element_type=F32)
    wg_ref[...] = grads[:hid].astype(BF16)
    wu_ref[...] = grads[hid : 2 * hid].astype(BF16)
    wd_ref[...] = grads[2 * hid :].astype(BF16)
    gt_ref[...] = jnp.dot(sel_ref[0], fin_ref[...], preferred_element_type=F32).astype(BF16)

    @pl.when(pl.program_id(0) == 0)
    def _():
        dots = jnp.dot(sel_ref[0], dots_ref[...], preferred_element_type=F32)
        gg_ref[...] = jnp.where(ids_ref[...] < experts, dots[:, : ids_ref.shape[1]], 0.0)


def local(tokens, grad_out, expert_ids, gate_weights, w_gate, w_up, w_down):
    flat_count = lax.axis_size(("expert", "dp"))
    experts = flat_count // SPAN
    count, features = tokens.shape
    hid = w_gate.shape[0]
    half = features // 2
    wide = features + LANE
    narrow = half + LANE
    slots = experts * SPAN
    far = max(experts - 1, 1)
    vmem = pl.BlockSpec(memory_space=pltpu.VMEM)
    anyspace = pl.BlockSpec(memory_space=pl.ANY)
    sem = pltpu.SemaphoreType.DMA
    buf, act, sel, fin = pl.pallas_call(
        functools.partial(exchange_kernel, experts),
        out_shape=(
            jax.ShapeDtypeStruct((slots, ROWS, wide), BF16),
            jax.ShapeDtypeStruct((slots, ROWS, 3 * hid), BF16),
            jax.ShapeDtypeStruct((2, count, experts * ROWS), BF16),
            jax.ShapeDtypeStruct((experts, ROWS, narrow), BF16),
        ),
        in_specs=[anyspace, anyspace, vmem, vmem, anyspace, anyspace, anyspace],
        out_specs=(vmem, vmem, vmem, vmem),
        scratch_shapes=[
            pltpu.VMEM((count, features), BF16),
            pltpu.VMEM((count, features), BF16),
            pltpu.VMEM((3 * hid, features), BF16),
            pltpu.VMEM((experts, ROWS, wide), BF16),
            pltpu.VMEM((slots, ROWS, narrow), BF16),
            pltpu.VMEM((experts, 4, ROWS, narrow), BF16),
            pltpu.VMEM((experts, 2, ROWS, narrow), BF16),
            pltpu.VMEM((experts, ROWS, narrow), BF16),
            sem((5,)),
            sem((far,)), sem((far,)),
            sem((experts,)), sem((experts,)),
            sem((experts,)), sem((experts,)),
            sem((experts,)), sem((experts,)),
            sem((experts, 4)), sem((experts, 4)),
            sem((experts, 4)), sem((experts, 4)),
            sem((experts, 2)), sem((experts, 2)),
            sem((experts,)), sem((experts,)),
            sem((far,)), sem((far,)),
        ],
        compiler_params=pltpu.CompilerParams(
            collective_id=0, has_side_effects=True, vmem_limit_bytes=56 * 1024 * 1024
        ),
    )(tokens, grad_out, expert_ids, gate_weights, w_gate, w_up, w_down)

    tiles = 4
    tile = features // tiles
    rows = slots * ROWS
    deep = experts * ROWS
    fin2 = fin.reshape(deep, narrow)
    wide_out = pl.BlockSpec((hid, tile), lambda t: (0, t))
    return pl.pallas_call(
        functools.partial(output_kernel, experts),
        grid=(tiles,),
        out_shape=(
            jax.ShapeDtypeStruct((count, features), BF16),
            jax.ShapeDtypeStruct(gate_weights.shape, F32),
            jax.ShapeDtypeStruct((hid, features), BF16),
            jax.ShapeDtypeStruct((hid, features), BF16),
            jax.ShapeDtypeStruct((hid, features), BF16),
        ),
        in_specs=[
            pl.BlockSpec((rows, tile), lambda t: (0, t)),
            pl.BlockSpec((rows, 3 * hid), lambda t: (0, 0)),
            pl.BlockSpec((1, count, deep), lambda t: (t // 2, 0, 0)),
            pl.BlockSpec((deep, tile), lambda t: (0, t % 2)),
            pl.BlockSpec((deep, LANE), lambda t: (0, half // LANE)),
            pl.BlockSpec(expert_ids.shape, lambda t: (0, 0)),
        ],
        out_specs=(
            pl.BlockSpec((count, tile), lambda t: (0, t)),
            pl.BlockSpec(gate_weights.shape, lambda t: (0, 0)),
            wide_out, wide_out, wide_out,
        ),
        compiler_params=pltpu.CompilerParams(vmem_limit_bytes=40 * 1024 * 1024),
    )(buf.reshape(rows, wide), act.reshape(rows, 3 * hid), sel, fin2, fin2, expert_ids)


def solution(mesh):
    rows = P(("groups", "expert", "dp"), None)
    weights = P(("expert", "dp"), None)
    return jax.shard_map(
        local,
        mesh=mesh,
        in_specs=(rows,) * 4 + (weights,) * 3,
        out_specs=(rows,) * 5,
        check_vma=False,
    )
```

time: 122 us -> 52.2 us (0.43)
  the two profiles are of different devices: /device:TPU:0 before, /device:TPU:4 now
where the time goes in v1:
time: 52.2 us; the launch traced here: 51.9 us
  Pallas kernels  43.5 us (83%)
  local copies, waits for them, and re-layouts  7.68 us (15%)
  between operations  0.66 us (1%)
    pallas_call x1, Pallas kernels, local(): pl.pallas_call(functools.partial(exchange_kernel, experts), out_shape=(ja...  39.9 us
    unnamed x12, local copies, waits for them, and re-layouts  7.02 us
    pallas_call x1, Pallas kernels, local(): pl.pallas_call(functools.partial(output_kernel, experts), grid=(tiles,),...  3.69 us

profile of v1, /device:TPU:4, one launch (start us, length us, event | category | flops | bytes accessed | tf_op | source)
XLA Modules:
  0.0 51.9 jit_solution(4576810023019324564)
XLA Ops:
  0.6 1.4 %copy.12.ids_ref = s32[128,8]{1,0:T(8,128)} copy(s32[128,8]{0,1:T(8,128)} %param.9) | data formatting | bytes 8192 | tf_op args[2]
  2.0 1.4 %copy.13.gates_ref = f32[128,8]{1,0:T(8,128)} copy(f32[128,8]{0,1:T(8,128)} %param.10) | data formatting | bytes 8192 | tf_op args[3]
  3.5 0.0 copy-start.1
  3.5 39.9 %shard_map.110 = (bf16[16,16,3712]{2,1,0:T(8,128)(2,1)}, bf16[16,16,384]{2,1,0:T(8,128)(2,1)}, bf16[2,128,32]{2,1,0:T(8,128)(2,1)}, bf16[2,16,1920]{2,1,0:T(8,128)(2,1)}) custom-call(bf16[128,3584]{1,0:T(8,128)(2,1)} %tokens_ref.1, bf16[128,3584]{1,0:T(8,128)(2,1)} %grad_ref.1, s32[128,8]{1,0:T(8,128)} %copy.12.ids_ref, f32[128,8]{1,0:T(8,128)} %copy.13.gates_ref, ...), custom_call_target="tpu_custom_call" | custom-call | tf_op jit(solution)/shard_map/pallas_call | solution.py:354
  43.3 0.0 copy-done.1
  43.3 0.0 copy-start
  43.4 1.5 %copy-done = bf16[16,16,3712]{2,1,0:T(8,128)(2,1)S(1)} copy-done((bf16[16,16,3712]{2,1,0:T(8,128)(2,1)S(1)}, bf16[16,16,3712]{2,1,0:T(8,128)(2,1)}, u32[]{:S(2)}) %copy-start) | copy-done | bytes 1900568
  44.9 0.0 copy-start.2
  44.9 0.9 %copy-done.2 = bf16[2,16,1920]{2,1,0:T(8,128)(2,1)S(1)} copy-done((bf16[2,16,1920]{2,1,0:T(8,128)(2,1)S(1)}, bf16[2,16,1920]{2,1,0:T(8,128)(2,1)}, u32[]{:S(2)}) %copy-start.2) | copy-done | bytes 122904
  45.8 0.0 copy-start.3
  45.8 0.9 %copy-done.3 = bf16[16,16,384]{2,1,0:T(8,128)(2,1)S(1)} copy-done((bf16[16,16,384]{2,1,0:T(8,128)(2,1)S(1)}, bf16[16,16,384]{2,1,0:T(8,128)(2,1)}, u32[]{:S(2)}) %copy-start.3) | copy-done | bytes 196632
  46.7 0.0 copy-start.4
  46.7 0.8 %copy-done.4 = bf16[2,128,32]{2,1,0:T(8,128)(2,1)S(1)} copy-done((bf16[2,128,32]{2,1,0:T(8,128)(2,1)S(1)}, bf16[2,128,32]{2,1,0:T(8,128)(2,1)}, u32[]{:S(2)}) %copy-start.4) | copy-done | bytes 16408
  47.5 3.7 %shard_map.111 = (bf16[128,3584]{1,0:T(8,128)(2,1)}, f32[128,8]{1,0:T(8,128)S(1)}, bf16[128,3584]{1,0:T(8,128)(2,1)}, bf16[128,3584]{1,0:T(8,128)(2,1)}, bf16[128,3584]{1,0:T(8,128)(2,1)}) custom-call(bf16[256,3712]{1,0:T(8,128)(2,1)S(1)} %bitcast.3, bf16[256,384]{1,0:T(8,128)(2,1)S(1)} %bitcast.6, bf16[2,128,32]{2,1,0:T(8,128)(2,1)S(1)} %copy-done.4, ...), custom_call_target="tpu_custom_call" | custom-call | tf_op jit(solution)/shard_map/pallas_call | solution.py:395
  51.2 0.7 %copy.15 = f32[128,8]{0,1:T(8,128)} copy(f32[128,8]{1,0:T(8,128)S(1)} %get-tuple-element.14) | data formatting | bytes 8192 | tf_op jit(solution)/shard_map/pallas_call | solution.py:395
Async XLA Ops:
  3.5 39.9 %copy-start.1 = (s32[128,8]{1,0:T(8,128)S(1)}, s32[128,8]{1,0:T(8,128)}, u32[]{:S(2)}) copy-start(s32[128,8]{1,0:T(8,128)} %copy.12.ids_ref) | copy-start | bytes 12292
  43.3 1.5 %copy-start = (bf16[16,16,3712]{2,1,0:T(8,128)(2,1)S(1)}, bf16[16,16,3712]{2,1,0:T(8,128)(2,1)}, u32[]{:S(2)}) copy-start(bf16[16,16,3712]{2,1,0:T(8,128)(2,1)} %get-tuple-element.9) | copy-start | bytes 5701636
  44.9 0.9 %copy-start.2 = (bf16[2,16,1920]{2,1,0:T(8,128)(2,1)S(1)}, bf16[2,16,1920]{2,1,0:T(8,128)(2,1)}, u32[]{:S(2)}) copy-start(bf16[2,16,1920]{2,1,0:T(8,128)(2,1)} %get-tuple-element.12) | copy-start | bytes 368644
  45.8 0.9 %copy-start.3 = (bf16[16,16,384]{2,1,0:T(8,128)(2,1)S(1)}, bf16[16,16,384]{2,1,0:T(8,128)(2,1)}, u32[]{:S(2)}) copy-start(bf16[16,16,384]{2,1,0:T(8,128)(2,1)} %get-tuple-element.10) | copy-start | bytes 589828
  46.7 0.8 %copy-start.4 = (bf16[2,128,32]{2,1,0:T(8,128)(2,1)S(1)}, bf16[2,128,32]{2,1,0:T(8,128)(2,1)}, u32[]{:S(2)}) copy-start(bf16[2,128,32]{2,1,0:T(8,128)(2,1)} %get-tuple-element.11.sel_ref) | copy-start | bytes 49156

commit v2 on v1

--- a/solution.py
+++ b/solution.py
@@ -28,9 +28,9 @@
 def exchange_kernel(
     experts,
     tokens_ref, grad_ref, ids_ref, gates_ref, wg_ref, wu_ref, wd_ref,
-    buf, act_ref, sel_ref, fin,
-    tok_v, dy_v, w_v, send, dxb, rc, r2, r1,
-    in_sem, s1_s, s1_r, a1_s, a1_r, a2_s, a2_r, a3_s, a3_r, ac_s, ac_r,
+    buf_out, tail_out, act_out, sel_ref, fin,
+    tok_v, dy_v, w_v, send, buf, tail, act, dxb, rc, r2, r1,
+    in_sem, out_sem, s1_s, s1_r, a1_s, a1_r, a2_s, a2_r, a3_s, a3_r, ac_s, ac_r,
     rc_s, rc_r, r2_s, r2_r, r1_s, r1_r, r0_s, r0_r,
 ):
     features = tok_v.shape[1]
@@ -71,48 +71,53 @@
     for copy in loads:
         copy.start()
 
-    count = ids_ref.shape[0]
-    width = experts * ROWS
-    lane = lax.broadcasted_iota(jnp.int32, (count, width), 1)
-    lane_expert = lane // ROWS
-    lane_row = lane % 8
-    lane_dy = (lane // 8) % 2
-    member = jnp.zeros((count, width), F32)
-    gate = jnp.zeros((count, width), F32)
-    for s in range(ids_ref.shape[1]):
-        hit = ids_ref[:, s : s + 1] == lane_expert
+    count = ids_ref.shape[1]
+    deep = experts * ROWS
+    row = lax.broadcasted_iota(jnp.int32, (deep, count), 0)
+    row_expert = row // ROWS
+    row_slot = row % 8
+    row_dy = (row // 8) % 2
+    member = jnp.zeros((deep, count), F32)
+    gate = jnp.zeros((deep, count), F32)
+    for s in range(ids_ref.shape[0]):
+        hit = ids_ref[s : s + 1, :] == row_expert
         member = member + jnp.where(hit, 1.0, 0.0)
-        gate = gate + jnp.where(hit, gates_ref[:, s : s + 1], 0.0)
-    lower = jnp.where(
+        gate = gate + jnp.where(hit, gates_ref[s : s + 1, :], 0.0)
+    upper = jnp.where(
         lax.broadcasted_iota(jnp.int32, (count, count), 0)
-        >= lax.broadcasted_iota(jnp.int32, (count, count), 1),
+        <= lax.broadcasted_iota(jnp.int32, (count, count), 1),
         1.0, 0.0,
     ).astype(BF16)
-    rank = jnp.dot(lower, member.astype(BF16), preferred_element_type=F32)
-    chosen = jnp.where(
-        (member > 0.5) & (rank == (lane_row + 1).astype(F32)) & (lane_row < CAP), 1.0, 0.0
-    )
-    sel_x = jnp.where(lane_dy == 0, chosen, 0.0)
-    sel_dy = jnp.where(lane_dy == 1, chosen, 0.0)
-    gate_hi = gate.astype(BF16).astype(F32)
-    gate_mix = (sel_x * gate_hi + sel_dy * (gate - gate_hi)).astype(BF16)
-    sel_x = sel_x.astype(BF16)
-    sel_dy = sel_dy.astype(BF16)
+    rank = jnp.dot(member.astype(BF16), upper, preferred_element_type=F32)
+
+    def choose(wanted):
+        chosen = jnp.where((member > 0.5) & (rank == wanted.astype(F32)), 1.0, 0.0)
+        return (
+            chosen,
+            jnp.where(row_dy == 0, chosen, 0.0).astype(BF16),
+            jnp.where(row_dy == 1, chosen, 0.0).astype(BF16),
+        )
+
+    chosen, sel_x, sel_dy = choose(jnp.where(row_slot < CAP, row_slot + 1, -1))
+    weight = jnp.sum(chosen * gate, axis=1, keepdims=True)
+    weight_hi = weight.astype(BF16).astype(F32)
+    row_gate = jnp.where(row_dy == 0, weight_hi, weight - weight_hi)
     sel_ref[0] = sel_x
     sel_ref[1] = sel_dy
-    send[:, :, features:] = (
-        lax.dot_general(gate_mix, jnp.ones((count, LANE), BF16), FIRST, preferred_element_type=F32)
-        .astype(BF16)
-        .reshape(experts, ROWS, LANE)
-    )
+    tile = features // 4
+    main = 3 * tile
+    send[:, :, main:] = jnp.broadcast_to(row_gate[:, :1], (deep, LANE)).astype(BF16).reshape(experts, ROWS, LANE)
     loads[0].wait()
     loads[1].wait()
-    tile = features // 4
-    for c in range(4):
+    for c in range(3):
         cols = pl.ds(c * tile, tile)
-        block = lax.dot_general(
-            sel_x, tok_v[:, cols], FIRST, preferred_element_type=F32
-        ) + lax.dot_general(sel_dy, dy_v[:, cols], FIRST, preferred_element_type=F32)
+        _, end_x, end_dy = choose(jnp.where(row_slot < CAP, -1, (row_slot - CAP) * 3 + c + 1))
+        block = (
+            jnp.dot(sel_x, tok_v[:, cols], preferred_element_type=F32)
+            + jnp.dot(sel_dy, dy_v[:, cols], preferred_element_type=F32)
+            + jnp.dot(end_x, tok_v[:, main:], preferred_element_type=F32)
+            + jnp.dot(end_dy, dy_v[:, main:], preferred_element_type=F32)
+        )
         send[:, :, cols] = block.astype(BF16).reshape(experts, ROWS, tile)
     buf[flat] = send[octet]
     pl.semaphore_wait(barrier, 3 + experts - 1)
@@ -185,32 +190,37 @@
         after_a2(i + 1)
 
     loop(experts - 1, rest)
-    loop(experts - 1, lambda i: after_a3(i + 1))
     for copy in loads[2:]:
         copy.wait()
 
-    def all_core(d):
+    deep_f = SPAN * ROWS
+    to_row = lax.broadcasted_iota(jnp.int32, (deep_f, deep_f), 0)
+    from_row = lax.broadcasted_iota(jnp.int32, (deep_f, deep_f), 1)
+    to_slot = to_row % 8
+    kept = (to_slot < CAP) & (from_row == (to_row // 8) * 8 + CAP + to_slot // 3)
+
+    def compute(d):
         for k in range(4):
             ac(d, k).wait_recv()
-
-    loop(experts, all_core)
-
-    def compute(f):
-        rows = pl.ds(f * SPAN, SPAN)
-        total = jnp.zeros((SPAN * ROWS, 3 * hid), F32)
-        for c in range(4):
+        rows = pl.ds(source(d) * SPAN, SPAN)
+        total = jnp.zeros((deep_f, 3 * hid), F32)
+        ends = jnp.zeros((deep_f, tile), F32)
+        for c in range(3):
             cols = pl.ds(c * tile, tile)
-            total = total + lax.dot_general(
-                buf[rows, :, cols].reshape(SPAN * ROWS, tile), w_v[:, cols], LAST,
-                preferred_element_type=F32,
-            )
+            piece = buf[rows, :, cols].reshape(deep_f, tile)
+            total = total + lax.dot_general(piece, w_v[:, cols], LAST, preferred_element_type=F32)
+            move = jnp.where(kept & (to_slot % 3 == c), 1.0, 0.0).astype(BF16)
+            ends = ends + jnp.dot(move, piece, preferred_element_type=F32)
+        ends = ends.astype(BF16)
+        tail[rows] = ends.reshape(SPAN, ROWS, tile)
+        total = total + lax.dot_general(ends, w_v[:, main:], LAST, preferred_element_type=F32)
         total = total.reshape(SPAN, 2, 8, 3 * hid)
         from_x = total[:, 0].reshape(SPAN * 8, 3 * hid)
         from_dy = total[:, 1].reshape(SPAN * 8, 3 * hid)
         pre_gate = from_x[:, :hid]
         pre_up = from_x[:, hid : 2 * hid]
         back = from_dy[:, 2 * hid :]
-        packed = buf[rows, :, pl.ds(features, LANE)].astype(F32)
+        packed = buf[rows, :, pl.ds(main, LANE)].astype(F32)
         weight = (packed[:, :8] + packed[:, 8:]).reshape(SPAN * 8, LANE)
         sig = jax.nn.sigmoid(pre_gate)
         silu = pre_gate * sig
@@ -223,7 +233,7 @@
         none = jnp.zeros((SPAN, 8, hid), F32)
         upper = jnp.concatenate([grad_gate.reshape(SPAN, 8, hid), grad_up.reshape(SPAN, 8, hid), none], axis=2)
         under = jnp.concatenate([none, none, down], axis=2)
-        act_ref[rows] = jnp.concatenate([upper, under], axis=1).astype(BF16)
+        act[rows] = jnp.concatenate([upper, under], axis=1).astype(BF16)
         pair = jnp.concatenate([grad_gate, grad_up], axis=1).astype(BF16)
         spread = jnp.broadcast_to(dots, (SPAN * 8, LANE)).reshape(SPAN, 8, LANE)
         dxb[rows, :, pl.ds(half, LANE)] = jnp.concatenate([spread, spread], axis=1).astype(BF16)
@@ -237,7 +247,6 @@
                 [left.reshape(SPAN, 8, step), right.reshape(SPAN, 8, step)], axis=1
             ).astype(BF16)
 
-    loop(experts, compute)
 
     partner_offsets = (0, second, first, first + second)
 
@@ -261,15 +270,28 @@
     def add(slot, piece):
         dxb[slot] = (dxb[slot].astype(F32) + piece.astype(F32)).astype(BF16)
 
-    def start_core(i):
-        d = experts - 1 - i
+    def start_core(d):
         for k in (2, 3, 1, 0):
             back_core(d, k).start()
 
-    loop(experts, start_core)
-
-    def sum_core(i):
-        d = experts - 1 - i
+    compute(0)
+    start_core(0)
+
+    def far_compute(i):
+        after_a3(i + 1)
+        compute(i + 1)
+        start_core(i + 1)
+
+    loop(experts - 1, far_compute)
+    stores = [
+        pltpu.make_async_copy(buf, buf_out, out_sem.at[0]),
+        pltpu.make_async_copy(tail, tail_out, out_sem.at[1]),
+        pltpu.make_async_copy(act, act_out, out_sem.at[2]),
+    ]
+    for copy in stores:
+        copy.start()
+
+    def sum_core(d):
         for k in (2, 3):
             back_core(d, k).wait_recv()
             add(base(d) + offsets[k], rc[d, k])
@@ -280,8 +302,7 @@
 
     loop(experts, sum_core)
 
-    def sum_second(i):
-        d = experts - 1 - i
+    def sum_second(d):
         back_second(d, 1).wait_recv()
         add(base(d) + first, r2[d, 1])
         back_first(d).start()
@@ -291,7 +312,7 @@
     loop(experts, sum_second)
 
     def sum_first(i):
-        d = experts - 1 - i
+        d = i + 1
         back_first(d).wait_recv()
         add(base(d), r1[d])
         home(d - 1).start()
@@ -319,23 +340,37 @@
         home(i).wait_send()
 
     loop(experts - 1, finish_far)
+    for copy in stores:
+        copy.wait()
 
 
 def output_kernel(
-    experts, buf_ref, act_ref, sel_ref, fin_ref, dots_ref, ids_ref,
+    experts, buf_ref, tail_ref, act_ref, sel_ref, fin_ref, dots_ref, ids_ref,
     gt_ref, gg_ref, wg_ref, wu_ref, wd_ref,
 ):
     hid = wg_ref.shape[0]
-    grads = lax.dot_general(act_ref[...], buf_ref[...], FIRST, preferred_element_type=F32)
-    wg_ref[...] = grads[:hid].astype(BF16)
-    wu_ref[...] = grads[hid : 2 * hid].astype(BF16)
-    wd_ref[...] = grads[2 * hid :].astype(BF16)
-    gt_ref[...] = jnp.dot(sel_ref[0], fin_ref[...], preferred_element_type=F32).astype(BF16)
-
-    @pl.when(pl.program_id(0) == 0)
+    step = pl.program_id(0)
+
+    def weights(rows):
+        grads = lax.dot_general(act_ref[...], rows, FIRST, preferred_element_type=F32)
+        wg_ref[...] = grads[:hid].astype(BF16)
+        wu_ref[...] = grads[hid : 2 * hid].astype(BF16)
+        wd_ref[...] = grads[2 * hid :].astype(BF16)
+
+    @pl.when(step < 3)
     def _():
-        dots = jnp.dot(sel_ref[0], dots_ref[...], preferred_element_type=F32)
-        gg_ref[...] = jnp.where(ids_ref[...] < experts, dots[:, : ids_ref.shape[1]], 0.0)
+        weights(buf_ref[...])
+
+    @pl.when(step == 3)
+    def _():
+        weights(tail_ref[...])
+
+    gt_ref[...] = lax.dot_general(sel_ref[0], fin_ref[...], FIRST, preferred_element_type=F32).astype(BF16)
+
+    @pl.when(step == 0)
+    def _():
+        dots = lax.dot_general(dots_ref[...], sel_ref[0], FIRST, preferred_element_type=F32)
+        gg_ref[...] = jnp.where(ids_ref[...] < experts, dots[: ids_ref.shape[0]], 0.0)
 
 
 def local(tokens, grad_out, expert_ids, gate_weights, w_gate, w_up, w_down):
@@ -344,33 +379,41 @@
     count, features = tokens.shape
     hid = w_gate.shape[0]
     half = features // 2
-    wide = features + LANE
+    tiles = 4
+    tile = features // tiles
+    wide = 3 * tile + LANE
+    deep = experts * ROWS
+    ids_t, gates_t = expert_ids.T, gate_weights.T
     narrow = half + LANE
     slots = experts * SPAN
     far = max(experts - 1, 1)
     vmem = pl.BlockSpec(memory_space=pltpu.VMEM)
     anyspace = pl.BlockSpec(memory_space=pl.ANY)
     sem = pltpu.SemaphoreType.DMA
-    buf, act, sel, fin = pl.pallas_call(
+    buf, tail, act, sel, fin = pl.pallas_call(
         functools.partial(exchange_kernel, experts),
         out_shape=(
             jax.ShapeDtypeStruct((slots, ROWS, wide), BF16),
+            jax.ShapeDtypeStruct((slots, ROWS, tile), BF16),
             jax.ShapeDtypeStruct((slots, ROWS, 3 * hid), BF16),
-            jax.ShapeDtypeStruct((2, count, experts * ROWS), BF16),
+            jax.ShapeDtypeStruct((2, deep, count), BF16),
             jax.ShapeDtypeStruct((experts, ROWS, narrow), BF16),
         ),
         in_specs=[anyspace, anyspace, vmem, vmem, anyspace, anyspace, anyspace],
-        out_specs=(vmem, vmem, vmem, vmem),
+        out_specs=(anyspace, anyspace, anyspace, vmem, vmem),
         scratch_shapes=[
             pltpu.VMEM((count, features), BF16),
             pltpu.VMEM((count, features), BF16),
             pltpu.VMEM((3 * hid, features), BF16),
             pltpu.VMEM((experts, ROWS, wide), BF16),
+            pltpu.VMEM((slots, ROWS, wide), BF16),
+            pltpu.VMEM((slots, ROWS, tile), BF16),
+            pltpu.VMEM((slots, ROWS, 3 * hid), BF16),
             pltpu.VMEM((slots, ROWS, narrow), BF16),
             pltpu.VMEM((experts, 4, ROWS, narrow), BF16),
             pltpu.VMEM((experts, 2, ROWS, narrow), BF16),
             pltpu.VMEM((experts, ROWS, narrow), BF16),
-            sem((5,)),
+            sem((5,)), sem((3,)),
             sem((far,)), sem((far,)),
             sem((experts,)), sem((experts,)),
             sem((experts,)), sem((experts,)),
@@ -384,39 +427,38 @@
         compiler_params=pltpu.CompilerParams(
             collective_id=0, has_side_effects=True, vmem_limit_bytes=56 * 1024 * 1024
         ),
-    )(tokens, grad_out, expert_ids, gate_weights, w_gate, w_up, w_down)
-
-    tiles = 4
-    tile = features // tiles
+    )(tokens, grad_out, ids_t, gates_t, w_gate, w_up, w_down)
+
     rows = slots * ROWS
-    deep = experts * ROWS
     fin2 = fin.reshape(deep, narrow)
     wide_out = pl.BlockSpec((hid, tile), lambda t: (0, t))
-    return pl.pallas_call(
+    grad_tokens, grad_gates, grad_gate, grad_up, grad_down = pl.pallas_call(
         functools.partial(output_kernel, experts),
         grid=(tiles,),
         out_shape=(
             jax.ShapeDtypeStruct((count, features), BF16),
-            jax.ShapeDtypeStruct(gate_weights.shape, F32),
+            jax.ShapeDtypeStruct(gates_t.shape, F32),
             jax.ShapeDtypeStruct((hid, features), BF16),
             jax.ShapeDtypeStruct((hid, features), BF16),
             jax.ShapeDtypeStruct((hid, features), BF16),
         ),
         in_specs=[
-            pl.BlockSpec((rows, tile), lambda t: (0, t)),
+            pl.BlockSpec((rows, tile), lambda t: (0, jnp.minimum(t, 2))),
+            pl.BlockSpec((rows, tile), lambda t: (0, 0)),
             pl.BlockSpec((rows, 3 * hid), lambda t: (0, 0)),
-            pl.BlockSpec((1, count, deep), lambda t: (t // 2, 0, 0)),
+            pl.BlockSpec((1, deep, count), lambda t: (t // 2, 0, 0)),
             pl.BlockSpec((deep, tile), lambda t: (0, t % 2)),
             pl.BlockSpec((deep, LANE), lambda t: (0, half // LANE)),
-            pl.BlockSpec(expert_ids.shape, lambda t: (0, 0)),
+            pl.BlockSpec(ids_t.shape, lambda t: (0, 0)),
         ],
         out_specs=(
             pl.BlockSpec((count, tile), lambda t: (0, t)),
-            pl.BlockSpec(gate_weights.shape, lambda t: (0, 0)),
+            pl.BlockSpec(gates_t.shape, lambda t: (0, 0)),
             wide_out, wide_out, wide_out,
         ),
-        compiler_params=pltpu.CompilerParams(vmem_limit_bytes=40 * 1024 * 1024),
-    )(buf.reshape(rows, wide), act.reshape(rows, 3 * hid), sel, fin2, fin2, expert_ids)
+        compiler_params=pltpu.CompilerParams(vmem_limit_bytes=60 * 1024 * 1024),
+    )(buf.reshape(rows, wide), tail.reshape(rows, tile), act.reshape(rows, 3 * hid), sel, fin2, fin2, ids_t)
+    return grad_tokens, grad_gates.T, grad_gate, grad_up, grad_down
 
 
 def solution(mesh):

time: 52.2 us -> 42.2 us (0.81)
  the two profiles are of different devices: /device:TPU:4 before, /device:TPU:0 now
where the time goes in v2:
time: 42.2 us; the launch traced here: 41.5 us
  Pallas kernels  40.9 us (97%)
  between operations  0.64 us (2%)
    pallas_call x1, Pallas kernels, local(): pl.pallas_call(functools.partial(exchange_kernel, experts), out_shape=(ja...  35 us
    pallas_call x1, Pallas kernels, local(): pl.pallas_call(functools.partial(output_kernel, experts), grid=(tiles,),...  5.84 us

profile of v2, /device:TPU:0, one launch (start us, length us, event | category | flops | bytes accessed | tf_op | source)
XLA Modules:
  0.0 41.5 jit_solution(1311574245410854288)
XLA Ops:
  0.6 35.0 %shard_map.110 = (bf16[16,16,2816]{2,1,0:T(8,128)(2,1)}, bf16[16,16,896]{2,1,0:T(8,128)(2,1)}, bf16[16,16,384]{2,1,0:T(8,128)(2,1)}, bf16[2,32,128]{2,1,0:T(8,128)(2,1)}, bf16[2,16,1920]{2,1,0:T(8,128)(2,1)}) custom-call(bf16[128,3584]{1,0:T(8,128)(2,1)} %tokens_ref.1, bf16[128,3584]{1,0:T(8,128)(2,1)} %grad_ref.1, s32[8,128]{1,0:T(8,128)} %bitcast.12, ...), custom_call_target="tpu_custom_call" | custom-call | tf_op jit(solution)/shard_map/pallas_call | solution.py:393
  35.7 5.8 %shard_map.111 = (bf16[128,3584]{1,0:T(8,128)(2,1)}, f32[8,128]{1,0:T(8,128)}, bf16[128,3584]{1,0:T(8,128)(2,1)}, bf16[128,3584]{1,0:T(8,128)(2,1)}, bf16[128,3584]{1,0:T(8,128)(2,1)}) custom-call(bf16[256,2816]{1,0:T(8,128)(2,1)} %bitcast.7, bf16[256,896]{1,0:T(8,128)(2,1)} %bitcast.10, bf16[256,384]{1,0:T(8,128)(2,1)} %bitcast.11, ...), custom_call_target="tpu_custom_call" | custom-call | tf_op jit(solution)/shard_map/pallas_call | solution.py:435

commit v3 on v2

--- a/solution.py
+++ b/solution.py
@@ -28,10 +28,10 @@
 def exchange_kernel(
     experts,
     tokens_ref, grad_ref, ids_ref, gates_ref, wg_ref, wu_ref, wd_ref,
-    buf_out, tail_out, act_out, sel_ref, fin,
-    tok_v, dy_v, w_v, send, buf, tail, act, dxb, rc, r2, r1,
-    in_sem, out_sem, s1_s, s1_r, a1_s, a1_r, a2_s, a2_r, a3_s, a3_r, ac_s, ac_r,
-    rc_s, rc_r, r2_s, r2_r, r1_s, r1_r, r0_s, r0_r,
+    gt_ref, gg_ref, gwg_out, gwu_out, gwd_out,
+    sel_ref, fin, grads_v, tok_v, dy_v, w_v, send, buf, tail, act, dxb, rc, r1,
+    in_sem, out_sem, s1_s, s1_r, a1_s, a1_r, ac_s, ac_r,
+    rc_s, rc_r, r1_s, r1_r, r0_s, r0_r,
 ):
     features = tok_v.shape[1]
     half = features // 2
@@ -42,17 +42,16 @@
     pos = flat % SPAN
     bit1 = (pos // 2) % 2
     bit2 = pos // 4
-    step2 = 2 - 4 * bit1
-    step4 = 4 - 8 * bit2
     step_c = 1 - 2 * dp
-    first = jnp.where(dp == 0, step4, step2)
-    second = jnp.where(dp == 0, step2, step4)
+    first = 2 - 4 * bit1
+    second = 4 - 8 * bit2
+    offsets = (0, first, second, first + second)
 
     def dev(index):
         return {"expert": index // 2, "dp": index % 2}
 
     barrier = pltpu.get_barrier_semaphore()
-    for step in (first, second, step_c):
+    for step in (first, second, first + second, step_c):
         pl.semaphore_signal(barrier, 1, device_id=dev(flat + step), device_id_type=pl.DeviceIdType.MESH)
 
     def greet(i):
@@ -120,7 +119,7 @@
         )
         send[:, :, cols] = block.astype(BF16).reshape(experts, ROWS, tile)
     buf[flat] = send[octet]
-    pl.semaphore_wait(barrier, 3 + experts - 1)
+    pl.semaphore_wait(barrier, 4 + experts - 1)
 
     def remote(src, dst, ssem, rsem, index):
         return pltpu.make_async_remote_copy(
@@ -141,24 +140,21 @@
     def base(d):
         return source(d) * SPAN + pos
 
-    def a1(d):
-        return pass_on(base(d), a1_s.at[d], a1_r.at[d], flat + first)
-
-    def a2(d):
-        return pass_on(base(d), a2_s.at[d], a2_r.at[d], flat + second)
-
-    def a3(d):
-        return pass_on(base(d) + first, a3_s.at[d], a3_r.at[d], flat + second)
-
-    offsets = (0, first, second, first + second)
+    def a1(d, k):
+        return pass_on(base(d), a1_s.at[d, k - 1], a1_r.at[d, k - 1], flat + offsets[k])
 
     def ac(d, k):
         return pass_on(base(d) + offsets[k], ac_s.at[d, k], ac_r.at[d, k], flat + step_c)
 
     def own(d):
-        a1(d).start()
-        a2(d).start()
+        for k in (3, 1, 2):
+            a1(d, k).start()
         ac(d, 0).start()
+
+    def to_core(d):
+        for k in (1, 2, 3):
+            a1(d, k).wait_recv()
+            ac(d, k).start()
 
     loop(experts - 1, lambda i: s1(i).start())
     own(0)
@@ -167,29 +163,8 @@
         s1(i).wait_recv()
         own(i + 1)
 
-    def after_a1(d):
-        a1(d).wait_recv()
-        a3(d).start()
-        ac(d, 1).start()
-
-    def after_a2(d):
-        a2(d).wait_recv()
-        ac(d, 2).start()
-
-    def after_a3(d):
-        a3(d).wait_recv()
-        ac(d, 3).start()
-
-    after_a1(0)
-    after_a2(0)
+    to_core(0)
     loop(experts - 1, after_s1)
-    after_a3(0)
-
-    def rest(i):
-        after_a1(i + 1)
-        after_a2(i + 1)
-
-    loop(experts - 1, rest)
     for copy in loads[2:]:
         copy.wait()
 
@@ -248,20 +223,15 @@
             ).astype(BF16)
 
 
-    partner_offsets = (0, second, first, first + second)
-
     def back_core(d, k):
         return remote(
-            dxb.at[base(d) + step_c + partner_offsets[k]], rc.at[d, k], rc_s.at[d, k], rc_r.at[d, k], flat + step_c
-        )
-
-    def back_second(d, k):
+            dxb.at[base(d) + step_c + offsets[k]], rc.at[d, k], rc_s.at[d, k], rc_r.at[d, k], flat + step_c
+        )
+
+    def back(d, k):
         return remote(
-            dxb.at[base(d) + second + (0, first)[k]], r2.at[d, k], r2_s.at[d, k], r2_r.at[d, k], flat + second
-        )
-
-    def back_first(d):
-        return remote(dxb.at[base(d) + first], r1.at[d], r1_s.at[d], r1_r.at[d], flat + first)
+            dxb.at[base(d) + offsets[k]], r1.at[d, k - 1], r1_s.at[d, k - 1], r1_r.at[d, k - 1], flat + offsets[k]
+        )
 
     def home(i):
         to = source(i + 1)
@@ -271,67 +241,79 @@
         dxb[slot] = (dxb[slot].astype(F32) + piece.astype(F32)).astype(BF16)
 
     def start_core(d):
-        for k in (2, 3, 1, 0):
+        for k in (3, 1, 2, 0):
             back_core(d, k).start()
+
+    def sum_core(d):
+        for k in (3, 1, 2, 0):
+            back_core(d, k).wait_recv()
+            add(base(d) + offsets[k], rc[d, k])
+            if k > 0:
+                back(d, k).start()
+
+    def sum_back(d):
+        for k in (1, 2, 3):
+            back(d, k).wait_recv()
+        pieces = dxb[base(d)].astype(F32)
+        for k in range(3):
+            pieces = pieces + r1[d, k].astype(F32)
+        return pieces.astype(BF16)
+
+    def weight_grads(c):
+        rows = buf[:, :, c * tile : (c + 1) * tile] if c < 3 else tail[...]
+        grads = lax.dot_general(
+            act[...].reshape(experts * deep_f, 3 * hid), rows.reshape(experts * deep_f, tile), FIRST,
+            preferred_element_type=F32,
+        )
+        grads_v[:, pl.ds(c * tile, tile)] = grads.astype(BF16)
 
     compute(0)
     start_core(0)
+    loop(experts - 1, lambda i: to_core(i + 1))
+    sum_core(0)
 
     def far_compute(i):
-        after_a3(i + 1)
         compute(i + 1)
         start_core(i + 1)
 
     loop(experts - 1, far_compute)
+    loop(experts - 1, lambda i: sum_core(i + 1))
+    weight_grads(0)
+    weight_grads(1)
+
+    def far_home(i):
+        dxb[base(i + 1)] = sum_back(i + 1)
+        home(i).start()
+
+    loop(experts - 1, far_home)
+    weight_grads(2)
+    weight_grads(3)
     stores = [
-        pltpu.make_async_copy(buf, buf_out, out_sem.at[0]),
-        pltpu.make_async_copy(tail, tail_out, out_sem.at[1]),
-        pltpu.make_async_copy(act, act_out, out_sem.at[2]),
+        pltpu.make_async_copy(grads_v.at[pl.ds(i * hid, hid)], out, out_sem.at[i])
+        for i, out in enumerate((gwg_out, gwu_out, gwd_out))
     ]
     for copy in stores:
         copy.start()
-
-    def sum_core(d):
-        for k in (2, 3):
-            back_core(d, k).wait_recv()
-            add(base(d) + offsets[k], rc[d, k])
-            back_second(d, k - 2).start()
-        for k in (1, 0):
-            back_core(d, k).wait_recv()
-            add(base(d) + offsets[k], rc[d, k])
-
-    loop(experts, sum_core)
-
-    def sum_second(d):
-        back_second(d, 1).wait_recv()
-        add(base(d) + first, r2[d, 1])
-        back_first(d).start()
-        back_second(d, 0).wait_recv()
-        add(base(d), r2[d, 0])
-
-    loop(experts, sum_second)
-
-    def sum_first(i):
-        d = i + 1
-        back_first(d).wait_recv()
-        add(base(d), r1[d])
-        home(d - 1).start()
-
-    loop(experts - 1, sum_first)
-    back_first(0).wait_recv()
-    fin[octet] = (dxb[flat].astype(F32) + r1[0].astype(F32)).astype(BF16)
+    fin[octet] = sum_back(0)
     loop(experts - 1, lambda i: home(i).wait_recv())
 
+    gathered = fin[...].reshape(deep, half + LANE)
+    step = half // 2
+    for h in range(2):
+        for c in range(2):
+            gt_ref[:, h * half + c * step : h * half + (c + 1) * step] = lax.dot_general(
+                sel_ref[h], gathered[:, c * step : (c + 1) * step], FIRST, preferred_element_type=F32
+            ).astype(BF16)
+    dots = lax.dot_general(gathered[:, half:], sel_ref[0], FIRST, preferred_element_type=F32)
+    gg_ref[...] = jnp.where(ids_ref[...] < experts, dots[: ids_ref.shape[0]], 0.0)
+
     def finish(d):
-        a1(d).wait_send()
-        a2(d).wait_send()
-        a3(d).wait_send()
-        back_first(d).wait_send()
         for k in range(4):
             ac(d, k).wait_send()
             back_core(d, k).wait_send()
-        for k in range(2):
-            back_second(d, k).wait_send()
+        for k in (1, 2, 3):
+            a1(d, k).wait_send()
+            back(d, k).wait_send()
 
     loop(experts, finish)
 
@@ -342,35 +324,6 @@
     loop(experts - 1, finish_far)
     for copy in stores:
         copy.wait()
-
-
-def output_kernel(
-    experts, buf_ref, tail_ref, act_ref, sel_ref, fin_ref, dots_ref, ids_ref,
-    gt_ref, gg_ref, wg_ref, wu_ref, wd_ref,
-):
-    hid = wg_ref.shape[0]
-    step = pl.program_id(0)
-
-    def weights(rows):
-        grads = lax.dot_general(act_ref[...], rows, FIRST, preferred_element_type=F32)
-        wg_ref[...] = grads[:hid].astype(BF16)
-        wu_ref[...] = grads[hid : 2 * hid].astype(BF16)
-        wd_ref[...] = grads[2 * hid :].astype(BF16)
-
-    @pl.when(step < 3)
-    def _():
-        weights(buf_ref[...])
-
-    @pl.when(step == 3)
-    def _():
-        weights(tail_ref[...])
-
-    gt_ref[...] = lax.dot_general(sel_ref[0], fin_ref[...], FIRST, preferred_element_type=F32).astype(BF16)
-
-    @pl.when(step == 0)
-    def _():
-        dots = lax.dot_general(dots_ref[...], sel_ref[0], FIRST, preferred_element_type=F32)
-        gg_ref[...] = jnp.where(ids_ref[...] < experts, dots[: ids_ref.shape[0]], 0.0)
 
 
 def local(tokens, grad_out, expert_ids, gate_weights, w_gate, w_up, w_down):
@@ -390,18 +343,20 @@
     vmem = pl.BlockSpec(memory_space=pltpu.VMEM)
     anyspace = pl.BlockSpec(memory_space=pl.ANY)
     sem = pltpu.SemaphoreType.DMA
-    buf, tail, act, sel, fin = pl.pallas_call(
+    full = jax.ShapeDtypeStruct((hid, features), BF16)
+    grad_tokens, grad_gates, grad_gate, grad_up, grad_down = pl.pallas_call(
         functools.partial(exchange_kernel, experts),
         out_shape=(
-            jax.ShapeDtypeStruct((slots, ROWS, wide), BF16),
-            jax.ShapeDtypeStruct((slots, ROWS, tile), BF16),
-            jax.ShapeDtypeStruct((slots, ROWS, 3 * hid), BF16),
-            jax.ShapeDtypeStruct((2, deep, count), BF16),
-            jax.ShapeDtypeStruct((experts, ROWS, narrow), BF16),
+            jax.ShapeDtypeStruct((count, features), BF16),
+            jax.ShapeDtypeStruct(gates_t.shape, F32),
+            full, full, full,
         ),
         in_specs=[anyspace, anyspace, vmem, vmem, anyspace, anyspace, anyspace],
-        out_specs=(anyspace, anyspace, anyspace, vmem, vmem),
+        out_specs=(vmem, vmem, anyspace, anyspace, anyspace),
         scratch_shapes=[
+            pltpu.VMEM((2, deep, count), BF16),
+            pltpu.VMEM((experts, ROWS, narrow), BF16),
+            pltpu.VMEM((3 * hid, features), BF16),
             pltpu.VMEM((count, features), BF16),
             pltpu.VMEM((count, features), BF16),
             pltpu.VMEM((3 * hid, features), BF16),
@@ -411,53 +366,19 @@
             pltpu.VMEM((slots, ROWS, 3 * hid), BF16),
             pltpu.VMEM((slots, ROWS, narrow), BF16),
             pltpu.VMEM((experts, 4, ROWS, narrow), BF16),
-            pltpu.VMEM((experts, 2, ROWS, narrow), BF16),
-            pltpu.VMEM((experts, ROWS, narrow), BF16),
-            sem((5,)), sem((3,)),
+            pltpu.VMEM((experts, 3, ROWS, narrow), BF16),
+            sem((7,)), sem((3,)),
             sem((far,)), sem((far,)),
-            sem((experts,)), sem((experts,)),
-            sem((experts,)), sem((experts,)),
-            sem((experts,)), sem((experts,)),
+            sem((experts, 3)), sem((experts, 3)),
             sem((experts, 4)), sem((experts, 4)),
             sem((experts, 4)), sem((experts, 4)),
-            sem((experts, 2)), sem((experts, 2)),
-            sem((experts,)), sem((experts,)),
+            sem((experts, 3)), sem((experts, 3)),
             sem((far,)), sem((far,)),
         ],
         compiler_params=pltpu.CompilerParams(
-            collective_id=0, has_side_effects=True, vmem_limit_bytes=56 * 1024 * 1024
+            collective_id=0, has_side_effects=True, vmem_limit_bytes=60 * 1024 * 1024
         ),
     )(tokens, grad_out, ids_t, gates_t, w_gate, w_up, w_down)
-
-    rows = slots * ROWS
-    fin2 = fin.reshape(deep, narrow)
-    wide_out = pl.BlockSpec((hid, tile), lambda t: (0, t))
-    grad_tokens, grad_gates, grad_gate, grad_up, grad_down = pl.pallas_call(
-        functools.partial(output_kernel, experts),
-        grid=(tiles,),
-        out_shape=(
-            jax.ShapeDtypeStruct((count, features), BF16),
-            jax.ShapeDtypeStruct(gates_t.shape, F32),
-            jax.ShapeDtypeStruct((hid, features), BF16),
-            jax.ShapeDtypeStruct((hid, features), BF16),
-            jax.ShapeDtypeStruct((hid, features), BF16),
-        ),
-        in_specs=[
-            pl.BlockSpec((rows, tile), lambda t: (0, jnp.minimum(t, 2))),
-            pl.BlockSpec((rows, tile), lambda t: (0, 0)),
-            pl.BlockSpec((rows, 3 * hid), lambda t: (0, 0)),
-            pl.BlockSpec((1, deep, count), lambda t: (t // 2, 0, 0)),
-            pl.BlockSpec((deep, tile), lambda t: (0, t % 2)),
-            pl.BlockSpec((deep, LANE), lambda t: (0, half // LANE)),
-            pl.BlockSpec(ids_t.shape, lambda t: (0, 0)),
-        ],
-        out_specs=(
-            pl.BlockSpec((count, tile), lambda t: (0, t)),
-            pl.BlockSpec(gates_t.shape, lambda t: (0, 0)),
-            wide_out, wide_out, wide_out,
-        ),
-        compiler_params=pltpu.CompilerParams(vmem_limit_bytes=60 * 1024 * 1024),
-    )(buf.reshape(rows, wide), tail.reshape(rows, tile), act.reshape(rows, 3 * hid), sel, fin2, fin2, ids_t)
     return grad_tokens, grad_gates.T, grad_gate, grad_up, grad_down
 
 

time: 42.2 us -> 39.9 us (0.945)
  Pallas kernels: 40.9 us -> 32.1 us
  local copies, waits for them, and re-layouts: 0 us -> 6.78 us
    unnamed x0 -> x13, local copies, waits for them, and re-layouts: none -> 6.78 us
    pallas_call x1 -> x0, Pallas kernels: 5.84 us -> none  [local(): pl.pallas_call(functools.partial(output_kernel, experts), grid=(tiles,),...]
    pallas_call x1, Pallas kernels: 35 us -> 32.1 us  [local(): pl.pallas_call(functools.partial(exchange_kernel, experts), out_shape=(ja...]
where the time goes in v3:
time: 39.9 us; the launch traced here: 39.6 us
  Pallas kernels  32.1 us (80%)
  local copies, waits for them, and re-layouts  6.78 us (17%)
  between operations  0.66 us (2%)
    pallas_call x1, Pallas kernels, local(): pl.pallas_call(functools.partial(exchange_kernel, experts), out_shape=(ja...  32.1 us
    unnamed x13, local copies, waits for them, and re-layouts  6.78 us

profile of v3, /device:TPU:0, one launch (start us, length us, event | category | flops | bytes accessed | tf_op | source)
XLA Modules:
  0.0 39.6 jit_solution(12209760642147417820)
XLA Ops:
  0.6 32.1 %shard_map.110 = (bf16[128,3584]{1,0:T(8,128)(2,1)}, f32[8,128]{1,0:T(8,128)}, bf16[128,3584]{1,0:T(8,128)(2,1)}, bf16[128,3584]{1,0:T(8,128)(2,1)}, bf16[128,3584]{1,0:T(8,128)(2,1)}) custom-call(bf16[128,3584]{1,0:T(8,128)(2,1)} %tokens_ref.1, bf16[128,3584]{1,0:T(8,128)(2,1)} %grad_ref.1, s32[8,128]{1,0:T(8,128)} %bitcast.3, f32[8,128]{1,0:T(8,128)} %bitcast.4, ...), custom_call_target="tpu_custom_call" | custom-call | tf_op jit(solution)/shard_map/pallas_call | solution.py:347
  32.8 0.0 copy-start.3
  32.8 0.0 copy-start.2
  32.8 2.2 %copy.17 = bf16[128,3584]{1,0:T(8,128)(2,1)} copy(bf16[128,3584]{1,0:T(8,128)(2,1)} %get-tuple-element.20) | data formatting | bytes 1835008
  35.1 0.0 copy-done.3
  35.1 0.6 %copy.18 = f32[128,8]{0,1:T(8,128)} copy(f32[128,8]{0,1:T(8,128)S(1)} %bitcast.5) | data formatting | bytes 8192
  35.6 0.0 copy-done.2
  35.6 0.0 copy-start.1
  35.7 0.9 %copy.19 = bf16[128,3584]{1,0:T(8,128)(2,1)} copy(bf16[128,3584]{1,0:T(8,128)(2,1)S(1)} %copy-done.2) | data formatting | bytes 1835008
  36.6 0.6 %copy-done.1 = bf16[128,3584]{1,0:T(8,128)(2,1)S(1)} copy-done((bf16[128,3584]{1,0:T(8,128)(2,1)S(1)}, bf16[128,3584]{1,0:T(8,128)(2,1)}, u32[]{:S(2)}) %copy-start.1) | copy-done | bytes 917528
  37.2 0.0 copy-start
  37.2 0.9 %copy.20 = bf16[128,3584]{1,0:T(8,128)(2,1)} copy(bf16[128,3584]{1,0:T(8,128)(2,1)S(1)} %copy-done.1) | data formatting | bytes 1835008
  38.1 0.6 %copy-done = bf16[128,3584]{1,0:T(8,128)(2,1)S(1)} copy-done((bf16[128,3584]{1,0:T(8,128)(2,1)S(1)}, bf16[128,3584]{1,0:T(8,128)(2,1)}, u32[]{:S(2)}) %copy-start) | copy-done | bytes 917528
  38.7 0.9 %copy.21 = bf16[128,3584]{1,0:T(8,128)(2,1)} copy(bf16[128,3584]{1,0:T(8,128)(2,1)S(1)} %copy-done) | data formatting | bytes 1835008
Async XLA Ops:
  32.8 2.3 %copy-start.3 = (f32[8,128]{1,0:T(8,128)S(1)}, f32[8,128]{1,0:T(8,128)}, u32[]{:S(2)}) copy-start(f32[8,128]{1,0:T(8,128)} %get-tuple-element.11) | copy-start | bytes 12292
  32.8 2.8 %copy-start.2 = (bf16[128,3584]{1,0:T(8,128)(2,1)S(1)}, bf16[128,3584]{1,0:T(8,128)(2,1)}, u32[]{:S(2)}) copy-start(bf16[128,3584]{1,0:T(8,128)(2,1)} %get-tuple-element.22) | copy-start | bytes 2752516
  35.6 1.5 %copy-start.1 = (bf16[128,3584]{1,0:T(8,128)(2,1)S(1)}, bf16[128,3584]{1,0:T(8,128)(2,1)}, u32[]{:S(2)}) copy-start(bf16[128,3584]{1,0:T(8,128)(2,1)} %get-tuple-element.23) | copy-start | bytes 2752516
  37.2 1.5 %copy-start = (bf16[128,3584]{1,0:T(8,128)(2,1)S(1)}, bf16[128,3584]{1,0:T(8,128)(2,1)}, u32[]{:S(2)}) copy-start(bf16[128,3584]{1,0:T(8,128)(2,1)} %get-tuple-element.24) | copy-start | bytes 2752516

commit v4 on v3

--- a/solution.py
+++ b/solution.py
@@ -326,6 +326,27 @@
         copy.wait()
 
 
+def hand_over_kernel(cuts, *refs):
+    count = len(cuts)
+    sources, results, held = refs[:count], refs[count : 2 * count], refs[2 * count : 3 * count]
+    in_sem, out_sem = refs[3 * count :]
+    arrive, leave = [], []
+    for i in range(count):
+        size = sources[i].shape[0] // cuts[i]
+        for c in range(cuts[i]):
+            rows = pl.ds(c * size, size)
+            n = len(arrive)
+            arrive.append(pltpu.make_async_copy(sources[i].at[rows], held[i].at[rows], in_sem.at[n]))
+            leave.append(pltpu.make_async_copy(held[i].at[rows], results[i].at[rows], out_sem.at[n]))
+    for copy in arrive:
+        copy.start()
+    for copy, after in zip(arrive, leave):
+        copy.wait()
+        after.start()
+    for copy in leave:
+        copy.wait()
+
+
 def local(tokens, grad_out, expert_ids, gate_weights, w_gate, w_up, w_down):
     flat_count = lax.axis_size(("expert", "dp"))
     experts = flat_count // SPAN
@@ -344,7 +365,7 @@
     anyspace = pl.BlockSpec(memory_space=pl.ANY)
     sem = pltpu.SemaphoreType.DMA
     full = jax.ShapeDtypeStruct((hid, features), BF16)
-    grad_tokens, grad_gates, grad_gate, grad_up, grad_down = pl.pallas_call(
+    made = pl.pallas_call(
         functools.partial(exchange_kernel, experts),
         out_shape=(
             jax.ShapeDtypeStruct((count, features), BF16),
@@ -379,6 +400,15 @@
             collective_id=0, has_side_effects=True, vmem_limit_bytes=60 * 1024 * 1024
         ),
     )(tokens, grad_out, ids_t, gates_t, w_gate, w_up, w_down)
+    cuts = (2, 1, 2, 2, 2)
+    grad_tokens, grad_gates, grad_gate, grad_up, grad_down = pl.pallas_call(
+        functools.partial(hand_over_kernel, cuts),
+        out_shape=tuple(jax.ShapeDtypeStruct(a.shape, a.dtype) for a in made),
+        in_specs=[anyspace] * len(cuts),
+        out_specs=(anyspace,) * len(cuts),
+        scratch_shapes=[pltpu.VMEM(a.shape, a.dtype) for a in made] + [sem((sum(cuts),)), sem((sum(cuts),))],
+        compiler_params=pltpu.CompilerParams(vmem_limit_bytes=60 * 1024 * 1024),
+    )(*made)
     return grad_tokens, grad_gates.T, grad_gate, grad_up, grad_down
 
 

time: 39.9 us -> 36.1 us (0.905)
  local copies, waits for them, and re-layouts: 6.78 us -> 0 us
  Pallas kernels: 32.1 us -> 35.3 us
    unnamed x13 -> x0, local copies, waits for them, and re-layouts: 6.78 us -> none
    pallas_call x0 -> x1, Pallas kernels: none -> 3.11 us  [local(): pl.pallas_call(functools.partial(hand_over_kernel, cuts), out_shape=tuple...]
where the time goes in v4:
time: 36.1 us; the launch traced here: 35.9 us
  Pallas kernels  35.3 us (98%)
  between operations  0.64 us (2%)
    pallas_call x1, Pallas kernels, local(): pl.pallas_call(functools.partial(exchange_kernel, experts), out_shape=(ja...  32.1 us
    pallas_call x1, Pallas kernels, local(): pl.pallas_call(functools.partial(hand_over_kernel, cuts), out_shape=tuple...  3.11 us

profile of v4, /device:TPU:0, one launch (start us, length us, event | category | flops | bytes accessed | tf_op | source)
XLA Modules:
  0.0 35.9 jit_solution(8370432886509334224)
XLA Ops:
  0.6 32.1 %shard_map.110 = (bf16[128,3584]{1,0:T(8,128)(2,1)}, f32[8,128]{1,0:T(8,128)}, bf16[128,3584]{1,0:T(8,128)(2,1)}, bf16[128,3584]{1,0:T(8,128)(2,1)}, bf16[128,3584]{1,0:T(8,128)(2,1)}) custom-call(bf16[128,3584]{1,0:T(8,128)(2,1)} %tokens_ref.1, bf16[128,3584]{1,0:T(8,128)(2,1)} %grad_ref.1, s32[8,128]{1,0:T(8,128)} %bitcast.3, f32[8,128]{1,0:T(8,128)} %bitcast.4, ...), custom_call_target="tpu_custom_call" | custom-call | tf_op jit(solution)/shard_map/pallas_call | solution.py:368
  32.8 3.1 %shard_map.111 = (bf16[128,3584]{1,0:T(8,128)(2,1)}, f32[8,128]{1,0:T(8,128)}, bf16[128,3584]{1,0:T(8,128)(2,1)}, bf16[128,3584]{1,0:T(8,128)(2,1)}, bf16[128,3584]{1,0:T(8,128)(2,1)}) custom-call(bf16[128,3584]{1,0:T(8,128)(2,1)} %get-tuple-element.15.refs_0_, f32[8,128]{1,0:T(8,128)} %get-tuple-element.16.refs_1_, ...), custom_call_target="tpu_custom_call" | custom-call | tf_op jit(solution)/shard_map/pallas_call | solution.py:404

commit v5 on v4

--- a/solution.py
+++ b/solution.py
@@ -130,41 +130,50 @@
     def source(d):
         return lax.rem(octet - d + experts, experts)
 
-    def s1(i):
+    part = (main + LANE) // 2
+    parts = (pl.ds(0, part), pl.ds(part, part))
+
+    def s1(i, p):
         other = lax.rem(octet + i + 1, experts)
-        return remote(send.at[other], buf.at[flat], s1_s.at[i], s1_r.at[i], other * SPAN + pos)
-
-    def pass_on(slot, ssem, rsem, index):
-        return remote(buf.at[slot], buf.at[slot], ssem, rsem, index)
+        return remote(
+            send.at[other, :, parts[p]], buf.at[flat, :, parts[p]], s1_s.at[i, p], s1_r.at[i, p], other * SPAN + pos
+        )
+
+    def pass_on(slot, p, ssem, rsem, index):
+        return remote(buf.at[slot, :, parts[p]], buf.at[slot, :, parts[p]], ssem, rsem, index)
 
     def base(d):
         return source(d) * SPAN + pos
 
-    def a1(d, k):
-        return pass_on(base(d), a1_s.at[d, k - 1], a1_r.at[d, k - 1], flat + offsets[k])
-
-    def ac(d, k):
-        return pass_on(base(d) + offsets[k], ac_s.at[d, k], ac_r.at[d, k], flat + step_c)
-
-    def own(d):
+    def a1(d, k, p):
+        return pass_on(base(d), p, a1_s.at[d, k - 1, p], a1_r.at[d, k - 1, p], flat + offsets[k])
+
+    def ac(d, k, p):
+        return pass_on(base(d) + offsets[k], p, ac_s.at[d, k, p], ac_r.at[d, k, p], flat + step_c)
+
+    def own(d, p):
         for k in (3, 1, 2):
-            a1(d, k).start()
-        ac(d, 0).start()
+            a1(d, k, p).start()
+        ac(d, 0, p).start()
 
     def to_core(d):
-        for k in (1, 2, 3):
-            a1(d, k).wait_recv()
-            ac(d, k).start()
-
-    loop(experts - 1, lambda i: s1(i).start())
-    own(0)
+        for p in range(2):
+            for k in (1, 2, 3):
+                a1(d, k, p).wait_recv()
+                ac(d, k, p).start()
+
+    for p in range(2):
+        loop(experts - 1, lambda i: s1(i, p).start())
+    own(0, 0)
+    own(0, 1)
 
     def after_s1(i):
-        s1(i).wait_recv()
-        own(i + 1)
-
+        for p in range(2):
+            s1(i, p).wait_recv()
+            own(i + 1, p)
+
+    loop(experts - 1, after_s1)
     to_core(0)
-    loop(experts - 1, after_s1)
     for copy in loads[2:]:
         copy.wait()
 
@@ -176,7 +185,8 @@
 
     def compute(d):
         for k in range(4):
-            ac(d, k).wait_recv()
+            for p in range(2):
+                ac(d, k, p).wait_recv()
         rows = pl.ds(source(d) * SPAN, SPAN)
         total = jnp.zeros((deep_f, 3 * hid), F32)
         ends = jnp.zeros((deep_f, tile), F32)
@@ -309,16 +319,19 @@
 
     def finish(d):
         for k in range(4):
-            ac(d, k).wait_send()
+            for p in range(2):
+                ac(d, k, p).wait_send()
             back_core(d, k).wait_send()
         for k in (1, 2, 3):
-            a1(d, k).wait_send()
+            for p in range(2):
+                a1(d, k, p).wait_send()
             back(d, k).wait_send()
 
     loop(experts, finish)
 
     def finish_far(i):
-        s1(i).wait_send()
+        for p in range(2):
+            s1(i, p).wait_send()
         home(i).wait_send()
 
     loop(experts - 1, finish_far)
@@ -389,9 +402,9 @@
             pltpu.VMEM((experts, 4, ROWS, narrow), BF16),
             pltpu.VMEM((experts, 3, ROWS, narrow), BF16),
             sem((7,)), sem((3,)),
-            sem((far,)), sem((far,)),
-            sem((experts, 3)), sem((experts, 3)),
-            sem((experts, 4)), sem((experts, 4)),
+            sem((far, 2)), sem((far, 2)),
+            sem((experts, 3, 2)), sem((experts, 3, 2)),
+            sem((experts, 4, 2)), sem((experts, 4, 2)),
             sem((experts, 4)), sem((experts, 4)),
             sem((experts, 3)), sem((experts, 3)),
             sem((far,)), sem((far,)),

time: 36.1 us -> 36.8 us (1.019)
  Pallas kernels: 35.3 us -> 36 us
    pallas_call x1, Pallas kernels: 32.1 us -> 32.9 us  [local(): pl.pallas_call(functools.partial(exchange_kernel, experts), out_shape=(ja...]
where the time goes in v5:
time: 36.8 us; the launch traced here: 36.6 us
  Pallas kernels  36 us (98%)
  between operations  0.64 us (2%)
    pallas_call x1, Pallas kernels, local(): pl.pallas_call(functools.partial(exchange_kernel, experts), out_shape=(ja...  32.9 us
    pallas_call x1, Pallas kernels, local(): pl.pallas_call(functools.partial(hand_over_kernel, cuts), out_shape=tuple...  3.11 us

profile of v5, /device:TPU:0, one launch (start us, length us, event | category | flops | bytes accessed | tf_op | source)
XLA Modules:
  0.0 36.6 jit_solution(17587802821757823043)
XLA Ops:
  0.6 32.9 %shard_map.110 = (bf16[128,3584]{1,0:T(8,128)(2,1)}, f32[8,128]{1,0:T(8,128)}, bf16[128,3584]{1,0:T(8,128)(2,1)}, bf16[128,3584]{1,0:T(8,128)(2,1)}, bf16[128,3584]{1,0:T(8,128)(2,1)}) custom-call(bf16[128,3584]{1,0:T(8,128)(2,1)} %tokens_ref.1, bf16[128,3584]{1,0:T(8,128)(2,1)} %grad_ref.1, s32[8,128]{1,0:T(8,128)} %bitcast.3, f32[8,128]{1,0:T(8,128)} %bitcast.4, ...), custom_call_target="tpu_custom_call" | custom-call | tf_op jit(solution)/shard_map/pallas_call | solution.py:381
  33.5 3.1 %shard_map.111 = (bf16[128,3584]{1,0:T(8,128)(2,1)}, f32[8,128]{1,0:T(8,128)}, bf16[128,3584]{1,0:T(8,128)(2,1)}, bf16[128,3584]{1,0:T(8,128)(2,1)}, bf16[128,3584]{1,0:T(8,128)(2,1)}) custom-call(bf16[128,3584]{1,0:T(8,128)(2,1)} %get-tuple-element.15.refs_0_, f32[8,128]{1,0:T(8,128)} %get-tuple-element.16.refs_1_, ...), custom_call_target="tpu_custom_call" | custom-call | tf_op jit(solution)/shard_map/pallas_call | solution.py:417
